TPU v7x, 256 devices: a whole 4x4x8 slice. The times are simulated.
256 devices in a mesh: dp: 256 (over y, z, x, core).
Axes of the slice: x: 4, y: 4, z: 8, core: 2. Of those that a mesh axis runs over, the one named last changes fastest.
Arguments:
- grads: bfloat16 [512, 1024, 1024], P('dp'), may hold values from -6 to 6
- memory: bfloat16 [512, 1024, 1024], P('dp'), may hold values from -6 to 6
- block_ids: int32 [16], replicated, may hold values from 0 to 63, as said below
- layer_ids: int32 [16], replicated, may hold values from 0 to 1, as said below
- master: float32 [128, 16384], P(None, 'dp'), may hold values from -8 to 8
- first_moment: float32 [128, 16384], P(None, 'dp'), may hold values from -8 to 8
- second_moment: float32 [128, 16384], P(None, 'dp'), may hold values from 0.25 to 4
Outputs:
- new_memory: bfloat16 [512, 1024, 1024], P('dp')
- master_new: float32 [128, 16384], P(None, 'dp')
- first_new: float32 [128, 16384], P(None, 'dp')
- second_new: float32 [128, 16384], P(None, 'dp')
- step_blocks: bfloat16 [16, 16384], replicated
Inputs may be any that keep to these rules, and one draw needn't show every extreme that they name: Block ids number the 64 tiles of a layer, and the pairs (layer_ids[k], block_ids[k]) are distinct. `layer_ids`: every layer is named by at least a quarter of the 16 entries, rounded down.
All inputs are finite; a program needn't handle non-finite values.
Results may differ from a plain program's by a relative error of at most 0.0004.
Values may be sent and summed in bfloat16 or wider, within the bound.
No kernel may reach another device: no remote copies, remote signals or barrier semaphores. Data moves between devices by JAX's collectives and lax.ppermute only.
A program may use at most 64 MiB of HBM per device.

v0:
```python
import jax
import jax.numpy as jnp
from jax import lax
from jax.sharding import PartitionSpec as P

TILE = 128


filter_rate = 0.3
beta_one = 0.9
beta_two = 0.999
adam_eps = 1e-06
weight_decay = 0.01
learn_rate = 0.01
norm_eps = 1e-06


def take_tiles(source, layer_ids, tile_row, tile_col):

    def single(layer_id, row_tile, col_tile):
        return lax.dynamic_slice(
            source, (layer_id, row_tile * TILE, col_tile * TILE), (1, TILE, TILE)
        )[0]

    return jax.vmap(single)(layer_ids, tile_row, tile_col)


def pack_blocks(grads_dev, memory_dev, layer_ids, tile_row, tile_col):
    grad_tiles = take_tiles(grads_dev, layer_ids, tile_row, tile_col).astype(jnp.float32)
    memory_tiles = take_tiles(memory_dev, layer_ids, tile_row, tile_col).astype(jnp.float32)
    combined = grad_tiles + memory_tiles
    return combined.reshape(combined.shape[0], TILE * TILE)


def selected_mask(layer_ids, block_ids, layers, tile_count):
    columns = layer_ids * (tile_count * tile_count) + block_ids
    all_columns = jnp.arange(layers * tile_count * tile_count, dtype=jnp.int32)
    chosen = jnp.any(columns[:, None] == all_columns[None, :], axis=0)
    return chosen.reshape(layers, tile_count, 1, tile_count, 1)


def filter_memory(grads_dev, memory_dev, chosen):
    layers, model_width, _ = grads_dev.shape
    tile_count = model_width // TILE
    accumulated = grads_dev.astype(jnp.float32) + memory_dev.astype(jnp.float32)
    shaped = accumulated.reshape(layers, tile_count, TILE, tile_count, TILE)
    filtered = jnp.where(chosen, jnp.float32(0.0), shaped).reshape(layers, model_width, model_width)
    mixed = (1.0 - filter_rate) * memory_dev.astype(jnp.float32) + filter_rate * filtered
    return mixed.astype(jnp.bfloat16)


def adam_rows(summed, weights_sel, first_old, second_old):
    first_sel = beta_one * first_old + (1.0 - beta_one) * summed
    second_sel = beta_two * second_old + (1.0 - beta_two) * summed * summed
    update = first_sel / (jnp.sqrt(second_sel) + adam_eps) + weight_decay * weights_sel
    return (first_sel, second_sel, update)


def layer_squares(member, values):
    return jnp.sum(member * jnp.sum(values * values, axis=1)[:, None], axis=0)


def trust_rows(member, weight_total, update_total):
    trust_ratio = jnp.sqrt(weight_total / (update_total + norm_eps))
    return jnp.sum(member * trust_ratio[None, :], axis=1)


def on_device(grads, memory, block_ids, layer_ids, master, first_moment, second_moment):
    layers, model_width, _ = grads.shape
    tile_count = model_width // TILE
    tile_row = block_ids // tile_count
    tile_col = block_ids % tile_count
    columns = layer_ids * (tile_count * tile_count) + block_ids
    member = (layer_ids[:, None] == jnp.arange(layers, dtype=jnp.int32)[None, :]).astype(
        jnp.float32
    )
    weights_sel = jnp.take(master, columns, axis=0)
    first_old = jnp.take(first_moment, columns, axis=0)
    second_old = jnp.take(second_moment, columns, axis=0)
    packed = pack_blocks(grads, memory, layer_ids, tile_row, tile_col)
    summed = lax.psum_scatter(packed, "dp", scatter_dimension=1, tiled=True)
    first_sel, second_sel, update = adam_rows(summed, weights_sel, first_old, second_old)
    weight_total, update_total = lax.psum(
        (layer_squares(member, weights_sel), layer_squares(member, update)), "dp"
    )
    scaled = trust_rows(member, weight_total, update_total)[:, None] * update
    step_blocks = lax.all_gather(scaled.astype(jnp.bfloat16), "dp", axis=1, tiled=True)
    new_memory = filter_memory(
        grads, memory, selected_mask(layer_ids, block_ids, layers, tile_count)
    )
    master_new = master.at[columns].set(weights_sel - learn_rate * scaled)
    first_new = first_moment.at[columns].set(first_sel)
    second_new = second_moment.at[columns].set(second_sel)
    return (new_memory, master_new, first_new, second_new, step_blocks)


def solution(mesh):
    in_specs = (
        P("dp", None, None),
        P("dp", None, None),
        P(),
        P(),
        P(None, "dp"),
        P(None, "dp"),
        P(None, "dp"),
    )
    out_specs = (P("dp", None, None), P(None, "dp"), P(None, "dp"), P(None, "dp"), P())
    return jax.shard_map(
        on_device, mesh=mesh, in_specs=in_specs, out_specs=out_specs, check_vma=False
    )
```

profile of v0, /device:TPU:1, one launch (start us, length us, event | category | flops | bytes accessed | tf_op | source)
XLA Modules:
  0.0 1558.2 jit_solution(10869497670686660173)
XLA Ops:
  8.0 56.4 %while.2 = (s32[]{:T(128)}, bf16[2,1024,1024]{2,1,0:T(8,128)(2,1)}, s32[16,3]{0,1:T(4,128)S(1)}, bf16[16,1,128,128]{3,2,1,0:T(8,128)(2,1)S(1)}, s32[]{:T(128)}) while((s32[]{:T(128)}, bf16[2,1024,1024]{2,1,0:T(8,128)(2,1)}, s32[16,3]{0,1:T(4,128)S(1)}, bf16[16,1,128,128]{3,2,1,0:T(8,128)(2,1)S(1)}, s32[]{:T(128)}) %tuple.52), condition=%wide.while_cond, body=%wide.while_body.sunk | while | flops 2 | bytes 65665 | solution.py:21
  8.6 2.9 bitcast_dynamic-update-slice_fusion.4
  15.7 2.9 bitcast_dynamic-update-slice_fusion.4
  19.2 2.9 bitcast_dynamic-update-slice_fusion.4
  29.8 2.9 bitcast_dynamic-update-slice_fusion.4
  33.3 2.9 bitcast_dynamic-update-slice_fusion.4
  43.9 2.9 bitcast_dynamic-update-slice_fusion.4
  54.4 2.9 bitcast_dynamic-update-slice_fusion.4
  57.9 2.9 bitcast_dynamic-update-slice_fusion.4
  61.5 2.9 bitcast_dynamic-update-slice_fusion.4
  64.5 56.4 %while.3 = (s32[]{:T(128)}, bf16[2,1024,1024]{2,1,0:T(8,128)(2,1)}, s32[16,3]{0,1:T(4,128)S(1)}, bf16[16,1,128,128]{3,2,1,0:T(8,128)(2,1)S(1)}, s32[]{:T(128)}) while((s32[]{:T(128)}, bf16[2,1024,1024]{2,1,0:T(8,128)(2,1)}, s32[16,3]{0,1:T(4,128)S(1)}, bf16[16,1,128,128]{3,2,1,0:T(8,128)(2,1)S(1)}, s32[]{:T(128)}) %tuple.57), condition=%wide.while_cond.1, body=%wide.while_body.1.sunk | while | flops 2 | bytes 65665 | solution.py:21
  65.1 2.9 bitcast_dynamic-update-slice_fusion.5
  72.2 2.9 bitcast_dynamic-update-slice_fusion.5
  75.7 2.9 bitcast_dynamic-update-slice_fusion.5
  86.3 2.9 bitcast_dynamic-update-slice_fusion.5
  89.8 2.9 bitcast_dynamic-update-slice_fusion.5
  100.3 2.9 bitcast_dynamic-update-slice_fusion.5
  107.3 2.9 bitcast_dynamic-update-slice_fusion.5
  121.1 4.6 copy.47
  130.0 5.3 broadcast_in_dim.52
  135.3 6.2 fusion.1
  141.5 1261.8 %reduce-scatter.4.cloned.1.call-done = f32[64,16]{1,0:T(8,128)} async-done(((f32[16384,16]{1,0:T(8,128)}), f32[64,16]{1,0:T(8,128)}) %reduce-scatter.4.cloned.1.call-update) | async-done | bytes 4112
  1404.5 78.2 %all-reduce = (f32[2]{0:T(128)S(1)}, f32[2]{0:T(128)S(1)}) all-reduce(f32[2]{0:T(128)S(1)} %get-tuple-element.38, f32[2]{0:T(128)S(1)} %get-tuple-element.37), channel_id=1, replica_groups=mesh['dp'=256] {'dp'}, use_global_device_ids=true, to_apply=%region_3.5 | all-reduce | flops 4 | bytes 32 | tf_op jit(solution)/shard_map/psum | solution.py:83
  1482.8 62.3 %all-gather = bf16[256,64,16]{1,2,0:T(8,128)(2,1)S(1)} all-gather(bf16[1,64,16]{1,2,0:T(8,128)(2,1)S(1)} %fusion.12), channel_id=1, replica_groups=mesh['dp'=256] {'dp'}, dimensions={0}, use_global_device_ids=true | all-gather | bytes 526336 | tf_op jit(solution)/shard_map/all_gather | solution.py:87
  (123 shorter events, 78.1 us)
Async XLA Ops:
  7.2 1396.1 %reduce-scatter.4.cloned.1.call-start = ((), (), s32[]{:S(2)}) async-start(), calls=%async_computation.1 | async-start | bytes 8421376
  121.1 4.7 copy-start
  121.1 4.8 copy-start.1
  121.1 4.9 copy-start.3
  121.1 4.9 copy-start.4
  121.1 6.1 copy-start.2
Sparse Core Ops, SparseCore 0:
  125.9 1277.3 reduce-scatter.3
where the time goes:
time: 1560 us
  waiting for transfers between devices  1260 us (81%)
  blocking collectives  140 us (9%)
  local copies, waits for them, and re-layouts  131 us (8%)
    unnamed x2, waiting for transfers between devices  1260 us
    gather x96, local copies, waits for them, and re-layouts  112 us
    psum x1, blocking collectives, on_device(): lax.psum((layer_squares(member, weights_sel), layer_squares(member, updat...  78.2 us
    all_gather x1, blocking collectives, on_device(): lax.all_gather(scaled.astype(jnp.bfloat16), 'dp', axis=1, tiled=True)  62.3 us
  transfers between devices with their start and end apart: 1, of which 1 were waited for; matrix products, arithmetic and copies ran while one was open for 1% of the time, Pallas kernels for 0%

commit v1 on v0

v1 whole, which is shorter than its diff:
```python
import functools

import jax
import jax.numpy as jnp
from jax import lax
from jax.experimental import pallas as pl
from jax.experimental.pallas import tpu as pltpu
from jax.sharding import Mesh
from jax.sharding import PartitionSpec as P

TILE = 128
SEL = 16
HALF = 64
Y, Z, X, C = 4, 8, 4, 2
YX = Y * X
TILES_SIDE = 8
BLOCKS_LAYER = 64

filter_rate = 0.3
beta_one = 0.9
beta_two = 0.999
adam_eps = 1e-06
weight_decay = 0.01
learn_rate = 0.01
norm_eps = 1e-06

f32 = jnp.float32
VMEM = pl.BlockSpec(memory_space=pltpu.VMEM)
SMEM = pl.BlockSpec(memory_space=pltpu.SMEM)
HBM = pl.BlockSpec(memory_space=pl.ANY)


def iota(shape, dim):
    return lax.broadcasted_iota(jnp.int32, shape, dim)


def one_hot(block_ref, layer_ref):
    sub = iota((SEL, 128), 0)
    column = jnp.zeros((SEL, 128), jnp.int32)
    for k in range(SEL):
        column = jnp.where(sub == k, layer_ref[k] * BLOCKS_LAYER + block_ref[k], column)
    return (column == iota((SEL, 128), 1)).astype(f32)


def layer_tile(layer_ref):
    sub = iota((8, 128), 0)
    low = iota((8, 128), 1) < HALF
    layer = jnp.zeros((8, 128), jnp.int32)
    for k in range(8):
        layer = jnp.where(sub == k, jnp.where(low, layer_ref[k], layer_ref[k + 8]), layer)
    return layer


def select_entries(hot, state):
    picked = lax.dot_general(
        hot, state, (((1,), (1,)), ((), ())), precision=lax.Precision.HIGHEST, preferred_element_type=f32
    )
    return jnp.concatenate([picked[:8], picked[8:]], axis=1)


def spread_entries(hot, tile):
    rows = jnp.concatenate([tile[:, :HALF], tile[:, HALF:]], axis=0)
    return lax.dot_general(
        rows, hot, (((0,), (0,)), ((), ())), precision=lax.Precision.HIGHEST, preferred_element_type=f32
    )


def pack_kernel(block_ref, layer_ref, grads, memory, keep_ref, send_ref, g_buf, m_buf, k_tmp, s_tmp, g_sem, m_sem):
    copies = []
    for k in (j + 8 * h for j in range(8) for h in range(2)):
        layer = layer_ref[k]
        row = pl.multiple_of((block_ref[k] // TILES_SIDE) * TILE, TILE)
        col = pl.multiple_of((block_ref[k] % TILES_SIDE) * TILE, TILE)
        at = (layer, pl.ds(row, TILE), pl.ds(col, TILE))
        for src, buf, sem in ((grads, g_buf, g_sem), (memory, m_buf, m_sem)):
            copy = pltpu.make_async_copy(src.at[at], buf.at[k], sem.at[k])
            copy.start()
            copies.append(copy)
    core = lax.axis_index("c")
    low = iota((TILE, TILE), 1) < HALF
    first_core = core == 0
    for j in range(8):
        for copy in copies[4 * j : 4 * j + 4]:
            copy.wait()
        a = g_buf[j].astype(f32) + m_buf[j].astype(f32)
        b = g_buf[j + 8].astype(f32) + m_buf[j + 8].astype(f32)
        for_first = jnp.where(low, a, pltpu.roll(b, HALF, 1))
        for_second = jnp.where(low, pltpu.roll(a, HALF, 1), b)
        k_tmp[j] = jnp.where(first_core, for_first, for_second)
        s_tmp[j] = jnp.where(first_core, for_second, for_first)
        for y in range(Y):
            for x in range(X):
                at = pl.ds((y * X + x) * 64 + j * 8, 8)
                rows = pl.ds(y * Z * X + x, Z, stride=X)
                keep_ref[at, :] = k_tmp[j, rows, :]
                send_ref[at, :] = s_tmp[j, rows, :]


def pack(block_ids, layer_ids, grads, memory):
    shape = jax.ShapeDtypeStruct((1024, 128), f32)
    return pl.pallas_call(
        pack_kernel,
        out_shape=(shape, shape),
        in_specs=[SMEM, SMEM, HBM, HBM],
        out_specs=(VMEM, VMEM),
        scratch_shapes=[
            pltpu.VMEM((SEL, TILE, TILE), jnp.bfloat16),
            pltpu.VMEM((SEL, TILE, TILE), jnp.bfloat16),
            pltpu.VMEM((8, TILE, TILE), f32),
            pltpu.VMEM((8, TILE, TILE), f32),
            pltpu.SemaphoreType.DMA((SEL,)),
            pltpu.SemaphoreType.DMA((SEL,)),
        ],
        cost_estimate=pl.CostEstimate(flops=10**6, bytes_accessed=2 << 20, transcendentals=0),
        name="pack_tiles",
    )(block_ids, layer_ids, grads, memory)


ROWS = 256


def filter_kernel(layer, block_ref, layer_ref, g_ref, m_ref, *rest):
    out_ref = rest[-1]
    step = pl.program_id(0)
    tile = iota((8, 1024), 1) // TILE
    for i in range(ROWS // TILE):
        first = (layer * TILES_SIDE + step * (ROWS // TILE) + i) * TILES_SIDE
        column = tile + first
        chosen = jnp.zeros((8, 1024), jnp.bool_)
        for k in range(SEL):
            chosen = jnp.logical_or(chosen, column == layer_ref[k] * BLOCKS_LAYER + block_ref[k])
        scale = jnp.where(chosen, f32(0.0), f32(1.0))[:1]
        for half in range(2):
            at = pl.ds(i * TILE + half * 64, 64)
            mem = m_ref[0, at, :].astype(f32)
            total = g_ref[0, at, :].astype(f32) + mem
            kept = jnp.where(scale > 0.5, total, f32(0.0))
            mixed = f32(1.0 - filter_rate) * mem + f32(filter_rate) * kept
            out_ref[0, at, :] = mixed.astype(jnp.bfloat16)


def filter_layer(layer, block_ids, layer_ids, grads, memory, into=None):
    spec = pl.BlockSpec((1, ROWS, 1024), lambda i, *_: (layer, i, 0))
    args = [block_ids, layer_ids, grads, memory]
    in_specs = [spec, spec]
    aliases = {}
    if into is not None:
        args.append(into)
        in_specs.append(HBM)
        aliases = {4: 0}
    return pl.pallas_call(
        functools.partial(filter_kernel, layer),
        out_shape=jax.ShapeDtypeStruct((2, 1024, 1024), jnp.bfloat16),
        grid_spec=pltpu.PrefetchScalarGridSpec(
            num_scalar_prefetch=2, grid=(1024 // ROWS,), in_specs=in_specs, out_specs=spec
        ),
        input_output_aliases=aliases,
        cost_estimate=pl.CostEstimate(flops=4 << 20, bytes_accessed=6 << 20, transcendentals=0),
        name="filter_memory",
    )(*args)


def moments_kernel(block_ref, layer_ref, master, first, second, out_ref):
    hot = one_hot(block_ref, layer_ref)
    for i, state in enumerate((first, second, master)):
        out_ref[pl.ds(8 * i, 8), :] = select_entries(hot, state[...])


def moments(block_ids, layer_ids, master, first, second):
    return pl.pallas_call(
        moments_kernel,
        out_shape=jax.ShapeDtypeStruct((24, 128), f32),
        in_specs=[SMEM, SMEM, VMEM, VMEM, VMEM],
        out_specs=VMEM,
        name="select_moments",
    )(block_ids, layer_ids, master, first, second)


def partial_kernel(got, own, out_ref, tmp):
    for j in range(8):
        total = got[0, pl.ds(8 * j, 8), :]
        for s in range(1, YX):
            total = total + got[s, pl.ds(8 * j, 8), :]
        tmp[pl.ds(j, Z, stride=8), :] = total
    for z in range(Z):
        out_ref[z, pl.ds(0, 64), :] = tmp[...]
        out_ref[z, pl.ds(64, 24), :] = own[...]


def partial_sums(got, own):
    return pl.pallas_call(
        partial_kernel,
        out_shape=jax.ShapeDtypeStruct((Z, 88, 128), f32),
        in_specs=[VMEM, VMEM],
        out_specs=VMEM,
        scratch_shapes=[pltpu.VMEM((64, 128), f32)],
        name="sum_partials",
    )(got, own)


def update_kernel(got, out_ref, own_sum, own_update):
    me = lax.axis_index("z")
    squares = jnp.zeros((8, 128), f32)
    for z in range(Z):
        at = pl.ds(8 * z, 8)
        summed = got[0, at, :]
        for s in range(1, Z):
            summed = summed + got[s, at, :]
        first = got[z, pl.ds(64, 8), :]
        second = got[z, pl.ds(72, 8), :]
        weights = got[z, pl.ds(80, 8), :]
        first_sel = beta_one * first + (1.0 - beta_one) * summed
        second_sel = beta_two * second + (1.0 - beta_two) * summed * summed
        update = first_sel / (jnp.sqrt(second_sel) + adam_eps) + weight_decay * weights
        squares = squares + weights * weights
        for s in range(YX):
            out_ref[s, at, :] = update

        @pl.when(me == z)
        def _():
            own_sum[...] = summed
            own_update[...] = update

    for s in range(YX):
        out_ref[s, pl.ds(64, 8), :] = squares


def updates(got):
    tile = jax.ShapeDtypeStruct((8, 128), f32)
    return pl.pallas_call(
        update_kernel,
        out_shape=(jax.ShapeDtypeStruct((YX, 72, 128), f32), tile, tile),
        in_specs=[VMEM],
        out_specs=(VMEM, VMEM, VMEM),
        name="lamb_update",
    )(got)


def state_kernel(block_ref, layer_ref, own_sum, first, second, first_new, second_new):
    hot = one_hot(block_ref, layer_ref)
    named = jnp.max(hot, axis=0, keepdims=True) > 0.5
    summed = spread_entries(hot, own_sum[...])
    old = first[...]
    first_new[...] = jnp.where(named, beta_one * old + (1.0 - beta_one) * summed, old)
    old = second[...]
    second_new[...] = jnp.where(named, beta_two * old + (1.0 - beta_two) * summed * summed, old)


def new_moments(block_ids, layer_ids, own_sum, first, second):
    state = jax.ShapeDtypeStruct((HALF, 128), f32)
    return pl.pallas_call(
        state_kernel,
        out_shape=(state, state),
        in_specs=[SMEM, SMEM, VMEM, VMEM, VMEM],
        out_specs=(VMEM, VMEM),
        name="new_moments",
    )(block_ids, layer_ids, own_sum, first, second)


def step_kernel(block_ref, layer_ref, own, other, own_update, master, step_ref, master_new):
    update_sq = jnp.zeros((8, 128), f32)
    weight_sq = jnp.zeros((8, 128), f32)
    for ref in (own, other):
        for s in range(YX):
            for z in range(Z):
                value = ref[s, pl.ds(8 * z, 8), :]
                update_sq = update_sq + value * value
            weight_sq = weight_sq + ref[s, pl.ds(64, 8), :]
    layer = layer_tile(layer_ref)
    ratio = jnp.zeros((8, 128), f32)
    for which in range(2):
        mine = layer == which
        weight_total = jnp.sum(jnp.where(mine, weight_sq, 0.0), keepdims=True)
        update_total = jnp.sum(jnp.where(mine, update_sq, 0.0), keepdims=True)
        ratio = jnp.where(mine, jnp.sqrt(weight_total / (update_total + norm_eps)), ratio)
    low = iota((8, 128), 1) < HALF

    def write(left, right):
        for y in range(Y):
            for x in range(X):
                for z in range(Z):
                    at = (y * X + x, pl.ds(8 * z, 8))
                    a = ratio * left[at]
                    b = ratio * right[at]
                    top = jnp.where(low, a, pltpu.roll(b, HALF, 1))
                    bottom = jnp.where(low, pltpu.roll(a, HALF, 1), b)
                    row = (y * Z + z) * X + x
                    step_ref[:, pl.ds(row * TILE, TILE)] = jnp.concatenate([top, bottom], axis=0).astype(
                        jnp.bfloat16
                    )

    core = lax.axis_index("c")
    pl.when(core == 0)(lambda: write(own, other))
    pl.when(core == 1)(lambda: write(other, own))
    hot = one_hot(block_ref, layer_ref)
    named = jnp.max(hot, axis=0, keepdims=True) > 0.5
    scaled = spread_entries(hot, ratio * own_update[...])
    old = master[...]
    master_new[...] = jnp.where(named, old - learn_rate * scaled, old)


def steps(block_ids, layer_ids, own, other, own_update, master):
    return pl.pallas_call(
        step_kernel,
        out_shape=(
            jax.ShapeDtypeStruct((SEL, TILE * TILE), jnp.bfloat16),
            jax.ShapeDtypeStruct((HALF, 128), f32),
        ),
        in_specs=[SMEM, SMEM, VMEM, VMEM, VMEM, VMEM],
        out_specs=(VMEM, VMEM),
        name="scaled_step",
    )(block_ids, layer_ids, own, other, own_update, master)


def on_device(grads, memory, block_ids, layer_ids, master, first_moment, second_moment):
    swap = [(0, 1), (1, 0)]
    master, first, second = master.T, first_moment.T, second_moment.T
    keep, send = pack(block_ids, layer_ids, grads, memory)
    received = lax.ppermute(send, "c", swap)
    new_memory = filter_layer(0, block_ids, layer_ids, grads, memory)
    own = moments(block_ids, layer_ids, master, first, second)
    part = (keep + received).reshape(YX, 64, 128)
    got = lax.all_to_all(part, ("y", "x"), 0, 0, tiled=True)
    got = lax.all_to_all(partial_sums(got, own), "z", 0, 0, tiled=True)
    payload, own_sum, own_update = updates(got)
    mine = lax.all_to_all(payload, ("y", "x"), 0, 0, tiled=True)
    other = lax.ppermute(mine, "c", swap)
    new_memory = filter_layer(1, block_ids, layer_ids, grads, memory, new_memory)
    first_new, second_new = new_moments(block_ids, layer_ids, own_sum, first, second)
    step_blocks, master_new = steps(block_ids, layer_ids, mine, other, own_update, master)
    return (new_memory, master_new.T, first_new.T, second_new.T, step_blocks)


def solution(mesh):
    torus = Mesh(mesh.devices.reshape(Y, Z, X, C), ("y", "z", "x", "c"))
    dp = ("y", "z", "x", "c")
    replica = P(dp, None, None)
    state = P(None, dp)
    return jax.shard_map(
        on_device,
        mesh=torus,
        in_specs=(replica, replica, P(), P(), state, state, state),
        out_specs=(replica, state, state, state, P()),
        check_vma=False,
    )
```

time: 1560 us -> 86.4 us (0.06)
  waiting for transfers between devices: 1260 us -> 10.7 us
  local copies, waits for them, and re-layouts: 131 us -> 1.62 us
  blocking collectives: 140 us -> 33.4 us
  Pallas kernels: 0 us -> 24.7 us
    unnamed x2 -> x0, waiting for transfers between devices: 1260 us -> none
    gather x99 -> x0, local copies, waits for them, and re-layouts: 114 us -> none
    psum x1 -> x0, blocking collectives: 78.2 us -> none  [on_device(): lax.psum((layer_squares(member, weights_sel), layer_squares(member, updat...]
    all_gather x1 -> x0, blocking collectives: 62.3 us -> none  [on_device(): lax.all_gather(scaled.astype(jnp.bfloat16), 'dp', axis=1, tiled=True)]
    all_to_all x0 -> x2, blocking collectives: none -> 33.4 us  [the longest x1 19.4 us: on_device(): got = lax.all_to_all(partial_sums(got, own), 'z', 0, 0, tiled=True)]
    pallas_call x0 -> x8, Pallas kernels: none -> 24.7 us  [the longest x2 10.8 us: filter_layer(): pl.pallas_call(functools.partial(filter_kernel, layer), out_shape=jax.Sha...]
  transfers between devices with their start and end apart: 1 -> 3, of which waited for: 1 -> 2; matrix products, arithmetic and copies ran while one was open for 1% -> 0% of each run, Pallas kernels for 0% -> 17%
where the time goes in v1:
time: 86.4 us; the launch traced here: 85.4 us
  blocking collectives  33.4 us (39%)
  Pallas kernels  24.7 us (29%)
  starting transfers between devices  12.5 us (14%)
  waiting for transfers between devices  10.7 us (12%)
  other arithmetic  1.91 us (2%)
  local copies, waits for them, and re-layouts  1.62 us (2%)
    all_to_all x1, blocking collectives, on_device(): got = lax.all_to_all(partial_sums(got, own), 'z', 0, 0, tiled=True)  19.4 us
    all_to_all x1, blocking collectives, on_device(): mine = lax.all_to_all(payload, ('y', 'x'), 0, 0, tiled=True)  14 us
    pallas_call x2, Pallas kernels, filter_layer(): pl.pallas_call(functools.partial(filter_kernel, layer), out_shape=jax.Sha...  10.8 us
    all_to_all x1, waiting for transfers between devices, on_device(): got = lax.all_to_all(part, ('y', 'x'), 0, 0, tiled=True)  8.96 us
    all_to_all x1, starting transfers between devices, on_device(): got = lax.all_to_all(part, ('y', 'x'), 0, 0, tiled=True)  5.02 us
    ppermute x1, starting transfers between devices, on_device(): other = lax.ppermute(mine, 'c', swap)  4.12 us
    pallas_call x1, Pallas kernels, pack(): pl.pallas_call(pack_kernel, out_shape=(shape, shape), in_specs=[SMEM, SME...  3.75 us
    ppermute x1, starting transfers between devices, on_device(): received = lax.ppermute(send, 'c', swap)  3.33 us
  transfers between devices with their start and end apart: 3, of which 2 were waited for; matrix products, arithmetic and copies ran while one was open for 0% of the time, Pallas kernels for 17%

profile of v1, /device:TPU:1, one launch (start us, length us, event | category | flops | bytes accessed | tf_op | source)
XLA Modules:
  0.0 85.4 jit_solution(16117546190018536920)
XLA Ops:
  0.6 3.8 %pack_tiles.1 = (f32[1024,128]{1,0:T(8,128)}, f32[1024,128]{1,0:T(8,128)}) custom-call(s32[16]{0:T(128)} %block_ref.11, s32[16]{0:T(128)} %layer_ref.11, bf16[2,1024,1024]{2,1,0:T(8,128)(2,1)} %grads.1, bf16[2,1024,1024]{2,1,0:T(8,128)(2,1)} %memory.1), custom_call_target="tpu_custom_call" | custom-call | flops 1000000 | bytes 2097152 | tf_op jit(solution)/shard_map/pack_tiles/pallas_call | solution.py:101
  4.4 3.3 %collective-permute-start = (f32[1024,128]{1,0:T(8,128)}, f32[1024,128]{1,0:T(8,128)S(1)}, u32[]{:S(2)}, u32[]{:S(2)}) collective-permute-start(f32[1024,128]{1,0:T(8,128)} %get-tuple-element.15), channel_id=1, source_target_pairs={{0,1},{1,0},{2,3},{3,2},{4,5},{5,4},{6,7},{7,6},{8,9},{9,8},{10,11... | collective-permute-start | bytes 1572872 | tf_op jit(solution)/shard_map/ppermute | solution.py:319
  7.7 1.7 %collective-permute-done = f32[1024,128]{1,0:T(8,128)S(1)} collective-permute-done((f32[1024,128]{1,0:T(8,128)}, f32[1024,128]{1,0:T(8,128)S(1)}, u32[]{:S(2)}, u32[]{:S(2)}) %collective-permute-start) | collective-permute-done | bytes 524320 | tf_op jit(solution)/shard_map/ppermute | solution.py:319
  9.5 1.9 %add.3 = f32[1024,128]{1,0:T(8,128)} add(f32[1024,128]{1,0:T(8,128)} %get-tuple-element.14, f32[1024,128]{1,0:T(8,128)S(1)} %collective-permute-done) | non-fusion elementwise | flops 131072 | bytes 1572864 | tf_op jit(solution)/shard_map/add | solution.py:322
  11.4 5.0 %all-to-all-start = ((f32[16,64,128]{2,1,0:T(8,128)}), f32[16,64,128]{2,1,0:T(8,128)S(1)}, u32[]{:S(2)}, u32[]{:S(2)}) async-start(f32[16,64,128]{2,1,0:T(8,128)} %bitcast), calls=%async_computation | async-start | bytes 1048576 | tf_op jit(solution)/shard_map/all_to_all | solution.py:323
  16.4 1.8 %select_moments.1.own = f32[24,128]{1,0:T(8,128)} custom-call(s32[16]{0:T(128)} %block_ref.11, s32[16]{0:T(128)} %layer_ref.11, f32[64,128]{1,0:T(8,128)} %bitcast.7, f32[64,128]{1,0:T(8,128)} %bitcast.9, f32[64,128]{1,0:T(8,128)} %bitcast.11), custom_call_target="tpu_custom_call" | custom-call | tf_op jit(solution)/shard_map/select_moments/pallas_call | solution.py:170
  18.2 9.0 %all-to-all-done.got = f32[16,64,128]{2,1,0:T(8,128)S(1)} async-done(((f32[16,64,128]{2,1,0:T(8,128)}), f32[16,64,128]{2,1,0:T(8,128)S(1)}, u32[]{:S(2)}, u32[]{:S(2)}) %all-to-all-start) | async-done | bytes 524320 | tf_op jit(solution)/shard_map/all_to_all | solution.py:323
  27.1 0.0 copy-start.1
  27.1 0.8 copy-done.1
  27.9 1.8 %sum_partials.1 = f32[8,88,128]{2,1,0:T(8,128)} custom-call(f32[16,64,128]{2,1,0:T(8,128)} %copy-done.1, f32[24,128]{1,0:T(8,128)} %select_moments.1.own), custom_call_target="tpu_custom_call" | custom-call | tf_op jit(solution)/shard_map/sum_partials/pallas_call | solution.py:191
  29.7 19.4 %all_to_all.15.got = f32[8,88,128]{2,1,0:T(8,128)} all-to-all(f32[8,88,128]{2,1,0:T(8,128)} %sum_partials.1), channel_id=1, replica_groups=mesh['y'=4,'z'=8,'x'=4,'c'=2] {'z'}, dimensions={0} | all-to-all | bytes 720896 | tf_op jit(solution)/shard_map/all_to_all | solution.py:324
  49.1 2.1 %lamb_update.1 = (f32[16,72,128]{2,1,0:T(8,128)}, f32[8,128]{1,0:T(8,128)}, f32[8,128]{1,0:T(8,128)}) custom-call(f32[8,88,128]{2,1,0:T(8,128)} %all_to_all.15.got), custom_call_target="tpu_custom_call" | custom-call | tf_op jit(solution)/shard_map/lamb_update/pallas_call | solution.py:230
  51.2 14.0 %all_to_all.16.own = f32[16,72,128]{2,1,0:T(8,128)S(1)} all-to-all(f32[16,72,128]{2,1,0:T(8,128)} %get-tuple-element.16), channel_id=1, replica_groups=mesh['y'=4,'z'=8,'x'=4,'c'=2] {'y','x'}, dimensions={0} | all-to-all | bytes 1179648 | tf_op jit(solution)/shard_map/all_to_all | solution.py:326
  65.2 0.0 copy-start
  65.2 4.1 %collective-permute-start.1 = (f32[16,72,128]{2,1,0:T(8,128)S(1)}, f32[16,72,128]{2,1,0:T(8,128)S(1)}, u32[]{:S(2)}, u32[]{:S(2)}) collective-permute-start(f32[16,72,128]{2,1,0:T(8,128)S(1)} %all_to_all.16.own), channel_id=1, source_target_pairs={{0,1},{1,0},{2,3},{3,2},{4,5},{5,4},{6,7},{7,6},{8,9},{9,8},{10,11... | collective-permute-start | bytes 1769480 | tf_op jit(solution)/shard_map/ppermute | solution.py:327
  69.3 5.4 %filter_memory.2.rest_0_ = bf16[2,1024,1024]{2,1,0:T(8,128)(2,1)} custom-call(s32[16]{0:T(128)} %block_ref.11, s32[16]{0:T(128)} %layer_ref.11, bf16[2,1024,1024]{2,1,0:T(8,128)(2,1)} %grads.1, bf16[2,1024,1024]{2,1,0:T(8,128)(2,1)} %memory.1), custom_call_target="tpu_custom_call" | custom-call | flops 4194304 | bytes 6291456 | tf_op jit(solution)/shard_map/filter_memory/pallas_call | solution.py:151
  74.7 0.0 copy-done
  74.7 5.4 %filter_memory.3 = bf16[2,1024,1024]{2,1,0:T(8,128)(2,1)} custom-call(s32[16]{0:T(128)} %block_ref.11, s32[16]{0:T(128)} %layer_ref.11, bf16[2,1024,1024]{2,1,0:T(8,128)(2,1)} %grads.1, bf16[2,1024,1024]{2,1,0:T(8,128)(2,1)} %memory.1, bf16[2,1024,1024]{2,1,0:T(8,128)(2,1)} %filter_memory.2.rest_0_), custom_call_target="tpu_custom_call", output_to_operand_aliasing={{}: (4, {})} | custom-call | flops 4194304 | bytes 6291456 | tf_op jit(solution)/shard_map/filter_memory/pallas_call | solution.py:151
  80.1 1.7 %new_moments.1 = (f32[64,128]{1,0:T(8,128)}, f32[64,128]{1,0:T(8,128)}) custom-call(s32[16]{0:T(128)} %block_ref.11, s32[16]{0:T(128)} %layer_ref.11, f32[8,128]{1,0:T(8,128)} %get-tuple-element.19.own_sum, f32[64,128]{1,0:T(8,128)} %bitcast.10, f32[64,128]{1,0:T(8,128)} %bitcast.12), custom_call_target="tpu_custom_call" | custom-call | tf_op jit(solution)/shard_map/new_moments/pallas_call | solution.py:251
  81.8 0.0 collective-permute-done.1.other
  81.8 0.0 copy-start.2
  81.8 0.8 copy-done.2
  82.7 2.8 %scaled_step.1 = (bf16[16,16384]{1,0:T(8,128)(2,1)}, f32[64,128]{1,0:T(8,128)}) custom-call(s32[16]{0:T(128)} %block_ref.11, s32[16]{0:T(128)} %layer_ref.11, f32[16,72,128]{2,1,0:T(8,128)} %copy-done, f32[16,72,128]{2,1,0:T(8,128)} %copy-done.2, f32[8,128]{1,0:T(8,128)} %get-tuple-element.17.own_update, f32[64,128]{1,0:T(8,128)} %bitcast.8), custom_call_target="tpu_custom_call" | custom-call | tf_op jit(solution)/shard_map/scaled_step/pallas_call | solution.py:303
Async XLA Ops:
  4.4 5.1 %collective-permute-start = (f32[1024,128]{1,0:T(8,128)}, f32[1024,128]{1,0:T(8,128)S(1)}, u32[]{:S(2)}, u32[]{:S(2)}) collective-permute-start(f32[1024,128]{1,0:T(8,128)} %get-tuple-element.15), channel_id=1, source_target_pairs={{0,1},{1,0},{2,3},{3,2},{4,5},{5,4},{6,7},{7,6},{8,9},{9,8},{10,11... | collective-permute-start | bytes 1572872 | tf_op jit(solution)/shard_map/ppermute | solution.py:319
  11.4 15.7 %all-to-all-start = ((f32[16,64,128]{2,1,0:T(8,128)}), f32[16,64,128]{2,1,0:T(8,128)S(1)}, u32[]{:S(2)}, u32[]{:S(2)}) async-start(f32[16,64,128]{2,1,0:T(8,128)} %bitcast), calls=%async_computation | async-start | bytes 1048576 | tf_op jit(solution)/shard_map/all_to_all | solution.py:323
  27.1 0.8 copy-start.1
  65.2 9.5 %copy-start = (f32[16,72,128]{2,1,0:T(8,128)}, f32[16,72,128]{2,1,0:T(8,128)S(1)}, u32[]{:S(2)}) copy-start(f32[16,72,128]{2,1,0:T(8,128)S(1)} %all_to_all.16.own) | copy-start | bytes 1769476
  65.2 16.6 %collective-permute-start.1 = (f32[16,72,128]{2,1,0:T(8,128)S(1)}, f32[16,72,128]{2,1,0:T(8,128)S(1)}, u32[]{:S(2)}, u32[]{:S(2)}) collective-permute-start(f32[16,72,128]{2,1,0:T(8,128)S(1)} %all_to_all.16.own), channel_id=1, source_target_pairs={{0,1},{1,0},{2,3},{3,2},{4,5},{5,4},{6,7},{7,6},{8,9},{9,8},{10,11... | collective-permute-start | bytes 1769480 | tf_op jit(solution)/shard_map/ppermute | solution.py:327
  81.8 0.8 copy-start.2

commit v2 on v1

--- a/solution.py
+++ b/solution.py
@@ -28,6 +28,12 @@
 VMEM = pl.BlockSpec(memory_space=pltpu.VMEM)
 SMEM = pl.BlockSpec(memory_space=pltpu.SMEM)
 HBM = pl.BlockSpec(memory_space=pl.ANY)
+LARGE = pltpu.CompilerParams(vmem_limit_bytes=16 << 20)
+SMALL = pltpu.CompilerParams(vmem_limit_bytes=8 << 20)
+
+
+def in_hbm(array):
+    return pltpu.with_memory_space_constraint(array, pltpu.HBM)
 
 
 def iota(shape, dim):
@@ -112,68 +118,80 @@
             pltpu.SemaphoreType.DMA((SEL,)),
         ],
         cost_estimate=pl.CostEstimate(flops=10**6, bytes_accessed=2 << 20, transcendentals=0),
+        compiler_params=SMALL,
         name="pack_tiles",
-    )(block_ids, layer_ids, grads, memory)
-
-
-ROWS = 256
-
-
-def filter_kernel(layer, block_ref, layer_ref, g_ref, m_ref, *rest):
-    out_ref = rest[-1]
-    step = pl.program_id(0)
-    tile = iota((8, 1024), 1) // TILE
-    for i in range(ROWS // TILE):
-        first = (layer * TILES_SIDE + step * (ROWS // TILE) + i) * TILES_SIDE
-        column = tile + first
-        chosen = jnp.zeros((8, 1024), jnp.bool_)
-        for k in range(SEL):
-            chosen = jnp.logical_or(chosen, column == layer_ref[k] * BLOCKS_LAYER + block_ref[k])
-        scale = jnp.where(chosen, f32(0.0), f32(1.0))[:1]
-        for half in range(2):
-            at = pl.ds(i * TILE + half * 64, 64)
-            mem = m_ref[0, at, :].astype(f32)
-            total = g_ref[0, at, :].astype(f32) + mem
-            kept = jnp.where(scale > 0.5, total, f32(0.0))
-            mixed = f32(1.0 - filter_rate) * mem + f32(filter_rate) * kept
-            out_ref[0, at, :] = mixed.astype(jnp.bfloat16)
-
-
-def filter_layer(layer, block_ids, layer_ids, grads, memory, into=None):
-    spec = pl.BlockSpec((1, ROWS, 1024), lambda i, *_: (layer, i, 0))
-    args = [block_ids, layer_ids, grads, memory]
-    in_specs = [spec, spec]
-    aliases = {}
-    if into is not None:
-        args.append(into)
-        in_specs.append(HBM)
-        aliases = {4: 0}
-    return pl.pallas_call(
-        functools.partial(filter_kernel, layer),
-        out_shape=jax.ShapeDtypeStruct((2, 1024, 1024), jnp.bfloat16),
-        grid_spec=pltpu.PrefetchScalarGridSpec(
-            num_scalar_prefetch=2, grid=(1024 // ROWS,), in_specs=in_specs, out_specs=spec
-        ),
-        input_output_aliases=aliases,
-        cost_estimate=pl.CostEstimate(flops=4 << 20, bytes_accessed=6 << 20, transcendentals=0),
-        name="filter_memory",
-    )(*args)
-
-
-def moments_kernel(block_ref, layer_ref, master, first, second, out_ref):
+    )(block_ids, layer_ids, in_hbm(grads), in_hbm(memory))
+
+
+PARTS = 8
+ROWS = 2 * 1024 // PARTS
+CHUNK = 16
+
+
+def filter_kernel(
+    block_ref, layer_ref, grads, memory, after, master, first, second, out, own, g_buf, m_buf, o_buf, g_sem, m_sem, o_sem
+):
+    def rows(part):
+        return pl.ds(pl.multiple_of(part * ROWS, ROWS), ROWS)
+
+    def read(part, src, buf, sem):
+        return pltpu.make_async_copy(src.at[rows(part)], buf.at[rows(part)], sem.at[part])
+
+    def write(part):
+        return pltpu.make_async_copy(o_buf.at[rows(part)], out.at[rows(part)], o_sem.at[part])
+
+    @pl.loop(0, PARTS)
+    def _(part):
+        read(part, grads, g_buf, g_sem).start()
+        read(part, memory, m_buf, m_sem).start()
+
     hot = one_hot(block_ref, layer_ref)
     for i, state in enumerate((first, second, master)):
-        out_ref[pl.ds(8 * i, 8), :] = select_entries(hot, state[...])
-
-
-def moments(block_ids, layer_ids, master, first, second):
-    return pl.pallas_call(
-        moments_kernel,
-        out_shape=jax.ShapeDtypeStruct((24, 128), f32),
-        in_specs=[SMEM, SMEM, VMEM, VMEM, VMEM],
-        out_specs=VMEM,
-        name="select_moments",
-    )(block_ids, layer_ids, master, first, second)
+        own[pl.ds(8 * i, 8), :] = select_entries(hot, state[...])
+    tile = iota((8, 1024), 1) // TILE
+
+    @pl.loop(0, PARTS)
+    def _(part):
+        read(part, grads, g_buf, g_sem).wait()
+        read(part, memory, m_buf, m_sem).wait()
+        for i in range(ROWS // TILE):
+            column = tile + (part * (ROWS // TILE) + i) * TILES_SIDE
+            chosen = jnp.zeros((8, 1024), jnp.bool_)
+            for k in range(SEL):
+                chosen = jnp.logical_or(chosen, column == layer_ref[k] * BLOCKS_LAYER + block_ref[k])
+            rate = jnp.where(chosen, f32(0.0), f32(filter_rate))
+            rate = jnp.concatenate([rate] * (CHUNK // 8), axis=0)
+
+            @pl.loop(0, TILE // CHUNK, unroll=TILE // CHUNK)
+            def _(c):
+                at = pl.ds(pl.multiple_of(part * ROWS + i * TILE + c * CHUNK, CHUNK), CHUNK)
+                mem = m_buf[at, :].astype(f32)
+                total = g_buf[at, :].astype(f32) + mem
+                mixed = f32(1.0 - filter_rate) * mem + rate * total
+                o_buf[at, :] = mixed.astype(jnp.bfloat16)
+
+        write(part).start()
+
+    @pl.loop(0, PARTS)
+    def _(part):
+        write(part).wait()
+
+
+def filter_memory(block_ids, layer_ids, grads, memory, after, master, first, second):
+    flat = (2 * 1024, 1024)
+    buf = pltpu.VMEM(flat, jnp.bfloat16)
+    sem = pltpu.SemaphoreType.DMA((PARTS,))
+    out, own = pl.pallas_call(
+        filter_kernel,
+        out_shape=(jax.ShapeDtypeStruct(flat, jnp.bfloat16), jax.ShapeDtypeStruct((24, 128), f32)),
+        in_specs=[SMEM, SMEM, HBM, HBM, HBM, VMEM, VMEM, VMEM],
+        out_specs=(HBM, VMEM),
+        scratch_shapes=[buf, buf, buf, sem, sem, sem],
+        compiler_params=LARGE,
+        cost_estimate=pl.CostEstimate(flops=8 << 20, bytes_accessed=12 << 20, transcendentals=0),
+        name="filter_memory",
+    )(block_ids, layer_ids, in_hbm(grads.reshape(flat)), in_hbm(memory.reshape(flat)), after, master, first, second)
+    return out.reshape(2, 1024, 1024), own
 
 
 def partial_kernel(got, own, out_ref, tmp):
@@ -194,6 +212,7 @@
         in_specs=[VMEM, VMEM],
         out_specs=VMEM,
         scratch_shapes=[pltpu.VMEM((64, 128), f32)],
+        compiler_params=SMALL,
         name="sum_partials",
     )(got, own)
 
@@ -232,6 +251,7 @@
         out_shape=(jax.ShapeDtypeStruct((YX, 72, 128), f32), tile, tile),
         in_specs=[VMEM],
         out_specs=(VMEM, VMEM, VMEM),
+        compiler_params=SMALL,
         name="lamb_update",
     )(got)
 
@@ -253,6 +273,7 @@
         out_shape=(state, state),
         in_specs=[SMEM, SMEM, VMEM, VMEM, VMEM],
         out_specs=(VMEM, VMEM),
+        compiler_params=SMALL,
         name="new_moments",
     )(block_ids, layer_ids, own_sum, first, second)
 
@@ -308,24 +329,25 @@
         ),
         in_specs=[SMEM, SMEM, VMEM, VMEM, VMEM, VMEM],
         out_specs=(VMEM, VMEM),
+        compiler_params=SMALL,
         name="scaled_step",
     )(block_ids, layer_ids, own, other, own_update, master)
 
 
 def on_device(grads, memory, block_ids, layer_ids, master, first_moment, second_moment):
     swap = [(0, 1), (1, 0)]
+    block_ids, layer_ids = in_hbm(block_ids), in_hbm(layer_ids)
     master, first, second = master.T, first_moment.T, second_moment.T
     keep, send = pack(block_ids, layer_ids, grads, memory)
     received = lax.ppermute(send, "c", swap)
-    new_memory = filter_layer(0, block_ids, layer_ids, grads, memory)
-    own = moments(block_ids, layer_ids, master, first, second)
     part = (keep + received).reshape(YX, 64, 128)
+    new_memory, own = filter_memory(block_ids, layer_ids, grads, memory, part, master, first, second)
     got = lax.all_to_all(part, ("y", "x"), 0, 0, tiled=True)
-    got = lax.all_to_all(partial_sums(got, own), "z", 0, 0, tiled=True)
+    sums = partial_sums(got, own)
+    got = lax.all_to_all(sums, "z", 0, 0, tiled=True)
     payload, own_sum, own_update = updates(got)
     mine = lax.all_to_all(payload, ("y", "x"), 0, 0, tiled=True)
     other = lax.ppermute(mine, "c", swap)
-    new_memory = filter_layer(1, block_ids, layer_ids, grads, memory, new_memory)
     first_new, second_new = new_moments(block_ids, layer_ids, own_sum, first, second)
     step_blocks, master_new = steps(block_ids, layer_ids, mine, other, own_update, master)
     return (new_memory, master_new.T, first_new.T, second_new.T, step_blocks)

time: 86.4 us -> 66.6 us (0.77)
  Pallas kernels: 24.7 us -> 13.4 us
  waiting for transfers between devices: 10.7 us -> 5.91 us
  local copies, waits for them, and re-layouts: 1.62 us -> 0.01 us
  other arithmetic: 1.91 us -> 0.85 us
    pallas_call x3 -> x1, Pallas kernels: 12.5 us -> 6.34 us  [filter_memory(): pl.pallas_call(filter_kernel, out_shape=(jax.ShapeDtypeStruct(flat, jnp.b...]
    all_to_all x1, waiting for transfers between devices: 8.96 us -> 4.33 us  [on_device(): got = lax.all_to_all(part, ('y', 'x'), 0, 0, tiled=True)]
    pallas_call x1, Pallas kernels: 2.07 us -> 0.26 us  [updates(): pl.pallas_call(update_kernel, out_shape=(jax.ShapeDtypeStruct((YX, 72, 12...]
    pallas_call x1, Pallas kernels: 1.83 us -> 0.06 us  [partial_sums(): pl.pallas_call(partial_kernel, out_shape=jax.ShapeDtypeStruct((Z, 88, 128...]
    unnamed x6, local copies, waits for them, and re-layouts: 1.62 us -> 0.01 us
    add x1, other arithmetic: 1.91 us -> 0.85 us  [on_device(): part = (keep + received).reshape(YX, 64, 128)]
  transfers between devices with their start and end apart: 3 -> 3, of which waited for: 2 -> 2; matrix products, arithmetic and copies ran while one was open for 0% -> 0% of each run, Pallas kernels for 17% -> 12%
where the time goes in v2:
time: 66.6 us; the launch traced here: 66.2 us
  blocking collectives  32.9 us (49%)
  Pallas kernels  13.4 us (20%)
  starting transfers between devices  12.5 us (19%)
  waiting for transfers between devices  5.91 us (9%)
  other arithmetic  0.85 us (1%)
  between operations  0.72 us (1%)
    all_to_all x1, blocking collectives, on_device(): got = lax.all_to_all(sums, 'z', 0, 0, tiled=True)  19.1 us
    all_to_all x1, blocking collectives, on_device(): mine = lax.all_to_all(payload, ('y', 'x'), 0, 0, tiled=True)  13.8 us
    pallas_call x1, Pallas kernels, filter_memory(): pl.pallas_call(filter_kernel, out_shape=(jax.ShapeDtypeStruct(flat, jnp.b...  6.34 us
    all_to_all x1, starting transfers between devices, on_device(): got = lax.all_to_all(part, ('y', 'x'), 0, 0, tiled=True)  5.02 us
    all_to_all x1, waiting for transfers between devices, on_device(): got = lax.all_to_all(part, ('y', 'x'), 0, 0, tiled=True)  4.33 us
    ppermute x1, starting transfers between devices, on_device(): other = lax.ppermute(mine, 'c', swap)  4.12 us
    ppermute x1, starting transfers between devices, on_device(): received = lax.ppermute(send, 'c', swap)  3.33 us
    pallas_call x1, Pallas kernels, pack(): pl.pallas_call(pack_kernel, out_shape=(shape, shape), in_specs=[SMEM, SME...  2.92 us
  transfers between devices with their start and end apart: 3, of which 2 were waited for; matrix products, arithmetic and copies ran while one was open for 0% of the time, Pallas kernels for 12%

profile of v2, /device:TPU:1, one launch (start us, length us, event | category | flops | bytes accessed | tf_op | source)
XLA Modules:
  0.0 66.2 jit_solution(3247592762625808172)
XLA Ops:
  0.6 0.0 copy-start
  0.6 0.0 copy-start.1
  0.7 0.0 copy-start.2
  0.7 2.9 %pack_tiles.1 = (f32[1024,128]{1,0:T(8,128)S(1)}, f32[1024,128]{1,0:T(8,128)S(1)}) custom-call(s32[16]{0:T(128)} %block_ref.7, s32[16]{0:T(128)} %layer_ref.7, bf16[2,1024,1024]{2,1,0:T(8,128)(2,1)} %grads.1, bf16[2,1024,1024]{2,1,0:T(8,128)(2,1)} %memory.1), custom_call_target="tpu_custom_call" | custom-call | flops 1000000 | bytes 2097152 | tf_op jit(solution)/shard_map/pack_tiles/pallas_call | solution.py:107
  3.6 3.3 %collective-permute-start = (f32[1024,128]{1,0:T(8,128)S(1)}, f32[1024,128]{1,0:T(8,128)S(1)}, u32[]{:S(2)}, u32[]{:S(2)}) collective-permute-start(f32[1024,128]{1,0:T(8,128)S(1)} %get-tuple-element.17), channel_id=1, source_target_pairs={{0,1},{1,0},{2,3},{3,2},{4,5},{5,4},{6,7},{7,6},{8,9},{9,8},{10,11... | collective-permute-start | bytes 1572872 | tf_op jit(solution)/shard_map/ppermute | solution.py:342
  6.9 1.5 %collective-permute-done = f32[1024,128]{1,0:T(8,128)S(1)} collective-permute-done((f32[1024,128]{1,0:T(8,128)S(1)}, f32[1024,128]{1,0:T(8,128)S(1)}, u32[]{:S(2)}, u32[]{:S(2)}) %collective-permute-start) | collective-permute-done | bytes 524320 | tf_op jit(solution)/shard_map/ppermute | solution.py:342
  8.5 0.8 %add.3 = f32[1024,128]{1,0:T(8,128)} add(f32[1024,128]{1,0:T(8,128)S(1)} %get-tuple-element.16, f32[1024,128]{1,0:T(8,128)S(1)} %collective-permute-done) | non-fusion elementwise | flops 131072 | bytes 1572864 | tf_op jit(solution)/shard_map/add | solution.py:343
  9.3 5.0 %all-to-all-start = ((f32[16,64,128]{2,1,0:T(8,128)}), f32[16,64,128]{2,1,0:T(8,128)S(1)}, u32[]{:S(2)}, u32[]{:S(2)}) async-start(f32[16,64,128]{2,1,0:T(8,128)} %bitcast.2.after), calls=%async_computation | async-start | bytes 1048576 | tf_op jit(solution)/shard_map/all_to_all | solution.py:345
  14.3 0.0 copy-done
  14.3 0.0 copy-done.1
  14.3 0.0 copy-done.2
  14.4 6.3 %filter_memory.1 = (bf16[2048,1024]{1,0:T(8,128)(2,1)}, f32[24,128]{1,0:T(8,128)S(1)}) custom-call(s32[16]{0:T(128)} %block_ref.7, s32[16]{0:T(128)} %layer_ref.7, bf16[2048,1024]{1,0:T(8,128)(2,1)} %bitcast.16, bf16[2048,1024]{1,0:T(8,128)(2,1)} %bitcast.17, f32[16,64,128]{2,1,0:T(8,128)} %bitcast.2.after, f32[64,128]{1,0:T(8,128)S(1)} %bitcast.10, ...), custom_call_target="tpu_custom_call" | custom-call | flops 8388608 | bytes 12582912 | tf_op jit(solution)/shard_map/filter_memory/pallas_call | solution.py:184
  20.7 4.3 %all-to-all-done.got = f32[16,64,128]{2,1,0:T(8,128)S(1)} async-done(((f32[16,64,128]{2,1,0:T(8,128)}), f32[16,64,128]{2,1,0:T(8,128)S(1)}, u32[]{:S(2)}, u32[]{:S(2)}) %all-to-all-start) | async-done | bytes 524320 | tf_op jit(solution)/shard_map/all_to_all | solution.py:345
  25.0 0.1 sum_partials.1
  25.1 19.1 %all_to_all.15.got = f32[8,88,128]{2,1,0:T(8,128)S(1)} all-to-all(f32[8,88,128]{2,1,0:T(8,128)S(1)} %sum_partials.1), channel_id=1, replica_groups=mesh['y'=4,'z'=8,'x'=4,'c'=2] {'z'}, dimensions={0} | all-to-all | bytes 720896 | tf_op jit(solution)/shard_map/all_to_all | solution.py:347
  44.2 0.3 lamb_update.1
  44.4 13.8 %all_to_all.16.own = f32[16,72,128]{2,1,0:T(8,128)S(1)} all-to-all(f32[16,72,128]{2,1,0:T(8,128)S(1)} %get-tuple-element.20), channel_id=1, replica_groups=mesh['y'=4,'z'=8,'x'=4,'c'=2] {'y','x'}, dimensions={0} | all-to-all | bytes 1179648 | tf_op jit(solution)/shard_map/all_to_all | solution.py:349
  58.2 4.1 %collective-permute-start.1 = (f32[16,72,128]{2,1,0:T(8,128)S(1)}, f32[16,72,128]{2,1,0:T(8,128)S(1)}, u32[]{:S(2)}, u32[]{:S(2)}) collective-permute-start(f32[16,72,128]{2,1,0:T(8,128)S(1)} %all_to_all.16.own), channel_id=1, source_target_pairs={{0,1},{1,0},{2,3},{3,2},{4,5},{5,4},{6,7},{7,6},{8,9},{9,8},{10,11... | collective-permute-start | bytes 1769480 | tf_op jit(solution)/shard_map/ppermute | solution.py:350
  62.4 1.6 %new_moments.1 = (f32[64,128]{1,0:T(8,128)}, f32[64,128]{1,0:T(8,128)}) custom-call(s32[16]{0:T(128)} %block_ref.7, s32[16]{0:T(128)} %layer_ref.7, f32[8,128]{1,0:T(8,128)S(1)} %get-tuple-element.23.own_sum, f32[64,128]{1,0:T(8,128)S(1)} %bitcast.13, f32[64,128]{1,0:T(8,128)S(1)} %bitcast.15), custom_call_target="tpu_custom_call" | custom-call | tf_op jit(solution)/shard_map/new_moments/pallas_call | solution.py:271
  63.9 0.0 collective-permute-done.1.other
  64.0 2.2 %scaled_step.1 = (bf16[16,16384]{1,0:T(8,128)(2,1)}, f32[64,128]{1,0:T(8,128)}) custom-call(s32[16]{0:T(128)} %block_ref.7, s32[16]{0:T(128)} %layer_ref.7, f32[16,72,128]{2,1,0:T(8,128)S(1)} %all_to_all.16.own, f32[16,72,128]{2,1,0:T(8,128)S(1)} %collective-permute-done.1.other, f32[8,128]{1,0:T(8,128)S(1)} %get-tuple-element.21.own_update, ...), custom_call_target="tpu_custom_call" | custom-call | tf_op jit(solution)/shard_map/scaled_step/pallas_call | solution.py:324
Async XLA Ops:
  0.6 13.7 %copy-start = (f32[128,64]{0,1:T(8,128)S(1)}, f32[128,64]{0,1:T(8,128)}, u32[]{:S(2)}) copy-start(f32[128,64]{0,1:T(8,128)} %param.11) | copy-start | bytes 98308
  0.6 13.7 %copy-start.1 = (f32[128,64]{0,1:T(8,128)S(1)}, f32[128,64]{0,1:T(8,128)}, u32[]{:S(2)}) copy-start(f32[128,64]{0,1:T(8,128)} %param.12) | copy-start | bytes 98308
  0.7 13.7 %copy-start.2 = (f32[128,64]{0,1:T(8,128)S(1)}, f32[128,64]{0,1:T(8,128)}, u32[]{:S(2)}) copy-start(f32[128,64]{0,1:T(8,128)} %param.13) | copy-start | bytes 98308
  3.6 4.9 %collective-permute-start = (f32[1024,128]{1,0:T(8,128)S(1)}, f32[1024,128]{1,0:T(8,128)S(1)}, u32[]{:S(2)}, u32[]{:S(2)}) collective-permute-start(f32[1024,128]{1,0:T(8,128)S(1)} %get-tuple-element.17), channel_id=1, source_target_pairs={{0,1},{1,0},{2,3},{3,2},{4,5},{5,4},{6,7},{7,6},{8,9},{9,8},{10,11... | collective-permute-start | bytes 1572872 | tf_op jit(solution)/shard_map/ppermute | solution.py:342
  9.3 15.7 %all-to-all-start = ((f32[16,64,128]{2,1,0:T(8,128)}), f32[16,64,128]{2,1,0:T(8,128)S(1)}, u32[]{:S(2)}, u32[]{:S(2)}) async-start(f32[16,64,128]{2,1,0:T(8,128)} %bitcast.2.after), calls=%async_computation | async-start | bytes 1048576 | tf_op jit(solution)/shard_map/all_to_all | solution.py:345
  58.2 5.8 %collective-permute-start.1 = (f32[16,72,128]{2,1,0:T(8,128)S(1)}, f32[16,72,128]{2,1,0:T(8,128)S(1)}, u32[]{:S(2)}, u32[]{:S(2)}) collective-permute-start(f32[16,72,128]{2,1,0:T(8,128)S(1)} %all_to_all.16.own), channel_id=1, source_target_pairs={{0,1},{1,0},{2,3},{3,2},{4,5},{5,4},{6,7},{7,6},{8,9},{9,8},{10,11... | collective-permute-start | bytes 1769480 | tf_op jit(solution)/shard_map/ppermute | solution.py:350

commit v3 on v2

--- a/solution.py
+++ b/solution.py
@@ -71,56 +71,80 @@
     )
 
 
-def pack_kernel(block_ref, layer_ref, grads, memory, keep_ref, send_ref, g_buf, m_buf, k_tmp, s_tmp, g_sem, m_sem):
+def half_columns(g_tiles, m_tiles, j, left):
+    low = iota((TILE, TILE), 1) < HALF
+    a = g_tiles[j].astype(f32) + m_tiles[j].astype(f32)
+    b = g_tiles[j + 8].astype(f32) + m_tiles[j + 8].astype(f32)
+    turned = pltpu.roll(jnp.where(left, b, a), HALF, 1)
+    return jnp.where(low, jnp.where(left, a, turned), jnp.where(left, turned, b))
+
+
+def store_rows(out_ref, tmp, j, value):
+    tmp[j] = value
+    for y in range(Y):
+        for x in range(X):
+            out_ref[pl.ds((y * X + x) * 64 + j * 8, 8), :] = tmp[j, pl.ds(y * Z * X + x, Z, stride=X), :]
+
+
+def send_kernel(block_ref, layer_ref, grads, memory, send_ref, g_tiles, m_tiles, tmp, g_sem, m_sem):
     copies = []
     for k in (j + 8 * h for j in range(8) for h in range(2)):
         layer = layer_ref[k]
         row = pl.multiple_of((block_ref[k] // TILES_SIDE) * TILE, TILE)
         col = pl.multiple_of((block_ref[k] % TILES_SIDE) * TILE, TILE)
         at = (layer, pl.ds(row, TILE), pl.ds(col, TILE))
-        for src, buf, sem in ((grads, g_buf, g_sem), (memory, m_buf, m_sem)):
+        for src, buf, sem in ((grads, g_tiles, g_sem), (memory, m_tiles, m_sem)):
             copy = pltpu.make_async_copy(src.at[at], buf.at[k], sem.at[k])
             copy.start()
             copies.append(copy)
-    core = lax.axis_index("c")
-    low = iota((TILE, TILE), 1) < HALF
-    first_core = core == 0
     for j in range(8):
         for copy in copies[4 * j : 4 * j + 4]:
             copy.wait()
-        a = g_buf[j].astype(f32) + m_buf[j].astype(f32)
-        b = g_buf[j + 8].astype(f32) + m_buf[j + 8].astype(f32)
-        for_first = jnp.where(low, a, pltpu.roll(b, HALF, 1))
-        for_second = jnp.where(low, pltpu.roll(a, HALF, 1), b)
-        k_tmp[j] = jnp.where(first_core, for_first, for_second)
-        s_tmp[j] = jnp.where(first_core, for_second, for_first)
-        for y in range(Y):
-            for x in range(X):
-                at = pl.ds((y * X + x) * 64 + j * 8, 8)
-                rows = pl.ds(y * Z * X + x, Z, stride=X)
-                keep_ref[at, :] = k_tmp[j, rows, :]
-                send_ref[at, :] = s_tmp[j, rows, :]
-
-
-def pack(block_ids, layer_ids, grads, memory):
-    shape = jax.ShapeDtypeStruct((1024, 128), f32)
-    return pl.pallas_call(
-        pack_kernel,
-        out_shape=(shape, shape),
+        store_rows(send_ref, tmp, j, half_columns(g_tiles, m_tiles, j, lax.axis_index("c") == 1))
+
+
+def keep_kernel(block_ref, layer_ref, g_tiles, m_tiles, master, first, second, keep_ref, own_ref, hot_ref, layers_ref, tmp):
+    for j in range(8):
+        store_rows(keep_ref, tmp, j, half_columns(g_tiles, m_tiles, j, lax.axis_index("c") == 0))
+    hot = one_hot(block_ref, layer_ref)
+    hot_ref[...] = hot
+    layers_ref[...] = layer_tile(layer_ref)
+    for i, state in enumerate((first, second, master)):
+        own_ref[pl.ds(8 * i, 8), :] = select_entries(hot, state[...])
+
+
+def pack_send(block_ids, layer_ids, grads, memory):
+    tiles = jax.ShapeDtypeStruct((SEL, TILE, TILE), jnp.bfloat16)
+    return pl.pallas_call(
+        send_kernel,
+        out_shape=(jax.ShapeDtypeStruct((1024, 128), f32), tiles, tiles),
         in_specs=[SMEM, SMEM, HBM, HBM],
-        out_specs=(VMEM, VMEM),
+        out_specs=(VMEM, VMEM, VMEM),
         scratch_shapes=[
-            pltpu.VMEM((SEL, TILE, TILE), jnp.bfloat16),
-            pltpu.VMEM((SEL, TILE, TILE), jnp.bfloat16),
-            pltpu.VMEM((8, TILE, TILE), f32),
             pltpu.VMEM((8, TILE, TILE), f32),
             pltpu.SemaphoreType.DMA((SEL,)),
             pltpu.SemaphoreType.DMA((SEL,)),
         ],
-        cost_estimate=pl.CostEstimate(flops=10**6, bytes_accessed=2 << 20, transcendentals=0),
-        compiler_params=SMALL,
-        name="pack_tiles",
+        compiler_params=SMALL,
+        name="pack_send",
     )(block_ids, layer_ids, in_hbm(grads), in_hbm(memory))
+
+
+def pack_keep(block_ids, layer_ids, g_tiles, m_tiles, master, first, second):
+    return pl.pallas_call(
+        keep_kernel,
+        out_shape=(
+            jax.ShapeDtypeStruct((1024, 128), f32),
+            jax.ShapeDtypeStruct((24, 128), f32),
+            jax.ShapeDtypeStruct((SEL, 128), f32),
+            jax.ShapeDtypeStruct((8, 128), jnp.int32),
+        ),
+        in_specs=[SMEM, SMEM, VMEM, VMEM, VMEM, VMEM, VMEM],
+        out_specs=(VMEM, VMEM, VMEM, VMEM),
+        scratch_shapes=[pltpu.VMEM((8, TILE, TILE), f32)],
+        compiler_params=SMALL,
+        name="pack_keep",
+    )(block_ids, layer_ids, g_tiles, m_tiles, master, first, second)
 
 
 PARTS = 8
@@ -129,7 +153,7 @@
 
 
 def filter_kernel(
-    block_ref, layer_ref, grads, memory, after, master, first, second, out, own, g_buf, m_buf, o_buf, g_sem, m_sem, o_sem
+    block_ref, layer_ref, grads, memory, after, out, done, g_buf, m_buf, o_buf, g_sem, m_sem, o_sem
 ):
     def rows(part):
         return pl.ds(pl.multiple_of(part * ROWS, ROWS), ROWS)
@@ -145,9 +169,7 @@
         read(part, grads, g_buf, g_sem).start()
         read(part, memory, m_buf, m_sem).start()
 
-    hot = one_hot(block_ref, layer_ref)
-    for i, state in enumerate((first, second, master)):
-        own[pl.ds(8 * i, 8), :] = select_entries(hot, state[...])
+    done[...] = jnp.zeros((8, 128), f32)
     tile = iota((8, 1024), 1) // TILE
 
     @pl.loop(0, PARTS)
@@ -177,24 +199,24 @@
         write(part).wait()
 
 
-def filter_memory(block_ids, layer_ids, grads, memory, after, master, first, second):
+def filter_memory(block_ids, layer_ids, grads, memory, after):
     flat = (2 * 1024, 1024)
     buf = pltpu.VMEM(flat, jnp.bfloat16)
     sem = pltpu.SemaphoreType.DMA((PARTS,))
-    out, own = pl.pallas_call(
+    out, done = pl.pallas_call(
         filter_kernel,
-        out_shape=(jax.ShapeDtypeStruct(flat, jnp.bfloat16), jax.ShapeDtypeStruct((24, 128), f32)),
-        in_specs=[SMEM, SMEM, HBM, HBM, HBM, VMEM, VMEM, VMEM],
+        out_shape=(jax.ShapeDtypeStruct(flat, jnp.bfloat16), jax.ShapeDtypeStruct((8, 128), f32)),
+        in_specs=[SMEM, SMEM, HBM, HBM, HBM],
         out_specs=(HBM, VMEM),
         scratch_shapes=[buf, buf, buf, sem, sem, sem],
         compiler_params=LARGE,
         cost_estimate=pl.CostEstimate(flops=8 << 20, bytes_accessed=12 << 20, transcendentals=0),
         name="filter_memory",
-    )(block_ids, layer_ids, in_hbm(grads.reshape(flat)), in_hbm(memory.reshape(flat)), after, master, first, second)
-    return out.reshape(2, 1024, 1024), own
-
-
-def partial_kernel(got, own, out_ref, tmp):
+    )(block_ids, layer_ids, in_hbm(grads.reshape(flat)), in_hbm(memory.reshape(flat)), after)
+    return out.reshape(2, 1024, 1024), done
+
+
+def partial_kernel(got, own, after, out_ref, tmp):
     for j in range(8):
         total = got[0, pl.ds(8 * j, 8), :]
         for s in range(1, YX):
@@ -205,16 +227,16 @@
         out_ref[z, pl.ds(64, 24), :] = own[...]
 
 
-def partial_sums(got, own):
+def partial_sums(got, own, after):
     return pl.pallas_call(
         partial_kernel,
         out_shape=jax.ShapeDtypeStruct((Z, 88, 128), f32),
-        in_specs=[VMEM, VMEM],
+        in_specs=[VMEM, VMEM, VMEM],
         out_specs=VMEM,
         scratch_shapes=[pltpu.VMEM((64, 128), f32)],
         compiler_params=SMALL,
         name="sum_partials",
-    )(got, own)
+    )(got, own, after)
 
 
 def update_kernel(got, out_ref, own_sum, own_update):
@@ -256,8 +278,8 @@
     )(got)
 
 
-def state_kernel(block_ref, layer_ref, own_sum, first, second, first_new, second_new):
-    hot = one_hot(block_ref, layer_ref)
+def state_kernel(hot_ref, own_sum, first, second, first_new, second_new):
+    hot = hot_ref[...]
     named = jnp.max(hot, axis=0, keepdims=True) > 0.5
     summed = spread_entries(hot, own_sum[...])
     old = first[...]
@@ -266,28 +288,33 @@
     second_new[...] = jnp.where(named, beta_two * old + (1.0 - beta_two) * summed * summed, old)
 
 
-def new_moments(block_ids, layer_ids, own_sum, first, second):
+def new_moments(hot, own_sum, first, second):
     state = jax.ShapeDtypeStruct((HALF, 128), f32)
     return pl.pallas_call(
         state_kernel,
         out_shape=(state, state),
-        in_specs=[SMEM, SMEM, VMEM, VMEM, VMEM],
+        in_specs=[VMEM] * 4,
         out_specs=(VMEM, VMEM),
         compiler_params=SMALL,
         name="new_moments",
-    )(block_ids, layer_ids, own_sum, first, second)
-
-
-def step_kernel(block_ref, layer_ref, own, other, own_update, master, step_ref, master_new):
-    update_sq = jnp.zeros((8, 128), f32)
+    )(hot, own_sum, first, second)
+
+
+CHUNKS = 4
+WIDTH = TILE * TILE // CHUNKS
+
+
+def step_kernel(layers_ref, hot_ref, own, other, own_update, master, step_ref, master_new, buf, sem):
+    update_sq = [jnp.zeros((8, 128), f32) for _ in range(4)]
     weight_sq = jnp.zeros((8, 128), f32)
     for ref in (own, other):
         for s in range(YX):
             for z in range(Z):
                 value = ref[s, pl.ds(8 * z, 8), :]
-                update_sq = update_sq + value * value
+                update_sq[z % 4] = update_sq[z % 4] + value * value
             weight_sq = weight_sq + ref[s, pl.ds(64, 8), :]
-    layer = layer_tile(layer_ref)
+    update_sq = (update_sq[0] + update_sq[1]) + (update_sq[2] + update_sq[3])
+    layer = layers_ref[...]
     ratio = jnp.zeros((8, 128), f32)
     for which in range(2):
         mine = layer == which
@@ -295,61 +322,64 @@
         update_total = jnp.sum(jnp.where(mine, update_sq, 0.0), keepdims=True)
         ratio = jnp.where(mine, jnp.sqrt(weight_total / (update_total + norm_eps)), ratio)
     low = iota((8, 128), 1) < HALF
-
-    def write(left, right):
-        for y in range(Y):
+    first_core = lax.axis_index("c") == 0
+
+    def chunk(i):
+        at = pl.ds(i * WIDTH, WIDTH)
+        return pltpu.make_async_copy(buf.at[:, at], step_ref.at[:, at], sem.at[i])
+
+    for y in range(Y):
+        for z in range(Z):
             for x in range(X):
-                for z in range(Z):
-                    at = (y * X + x, pl.ds(8 * z, 8))
-                    a = ratio * left[at]
-                    b = ratio * right[at]
-                    top = jnp.where(low, a, pltpu.roll(b, HALF, 1))
-                    bottom = jnp.where(low, pltpu.roll(a, HALF, 1), b)
-                    row = (y * Z + z) * X + x
-                    step_ref[:, pl.ds(row * TILE, TILE)] = jnp.concatenate([top, bottom], axis=0).astype(
-                        jnp.bfloat16
-                    )
-
-    core = lax.axis_index("c")
-    pl.when(core == 0)(lambda: write(own, other))
-    pl.when(core == 1)(lambda: write(other, own))
-    hot = one_hot(block_ref, layer_ref)
+                at = (y * X + x, pl.ds(8 * z, 8))
+                a = ratio * own[at]
+                b = ratio * other[at]
+                turned = pltpu.roll(jnp.where(first_core, b, a), HALF, 1)
+                straight = jnp.where(first_core, a, b)
+                top = jnp.where(low, straight, turned)
+                bottom = jnp.where(low, pltpu.roll(straight, HALF, 1), jnp.where(first_core, b, a))
+                row = (y * Z + z) * X + x
+                buf[:, pl.ds(row * TILE, TILE)] = jnp.concatenate([top, bottom], axis=0).astype(jnp.bfloat16)
+        chunk(y).start()
+    hot = hot_ref[...]
     named = jnp.max(hot, axis=0, keepdims=True) > 0.5
     scaled = spread_entries(hot, ratio * own_update[...])
     old = master[...]
     master_new[...] = jnp.where(named, old - learn_rate * scaled, old)
-
-
-def steps(block_ids, layer_ids, own, other, own_update, master):
+    for i in range(CHUNKS):
+        chunk(i).wait()
+
+
+def steps(layers, hot, own, other, own_update, master):
+    step = (SEL, TILE * TILE)
     return pl.pallas_call(
         step_kernel,
-        out_shape=(
-            jax.ShapeDtypeStruct((SEL, TILE * TILE), jnp.bfloat16),
-            jax.ShapeDtypeStruct((HALF, 128), f32),
-        ),
-        in_specs=[SMEM, SMEM, VMEM, VMEM, VMEM, VMEM],
-        out_specs=(VMEM, VMEM),
+        out_shape=(jax.ShapeDtypeStruct(step, jnp.bfloat16), jax.ShapeDtypeStruct((HALF, 128), f32)),
+        in_specs=[VMEM] * 6,
+        out_specs=(HBM, VMEM),
+        scratch_shapes=[pltpu.VMEM(step, jnp.bfloat16), pltpu.SemaphoreType.DMA((CHUNKS,))],
         compiler_params=SMALL,
         name="scaled_step",
-    )(block_ids, layer_ids, own, other, own_update, master)
+    )(layers, hot, own, other, own_update, master)
 
 
 def on_device(grads, memory, block_ids, layer_ids, master, first_moment, second_moment):
     swap = [(0, 1), (1, 0)]
     block_ids, layer_ids = in_hbm(block_ids), in_hbm(layer_ids)
     master, first, second = master.T, first_moment.T, second_moment.T
-    keep, send = pack(block_ids, layer_ids, grads, memory)
+    send, g_tiles, m_tiles = pack_send(block_ids, layer_ids, grads, memory)
     received = lax.ppermute(send, "c", swap)
+    keep, own, hot, layers = pack_keep(block_ids, layer_ids, g_tiles, m_tiles, master, first, second)
     part = (keep + received).reshape(YX, 64, 128)
-    new_memory, own = filter_memory(block_ids, layer_ids, grads, memory, part, master, first, second)
+    new_memory, done = filter_memory(block_ids, layer_ids, grads, memory, part)
     got = lax.all_to_all(part, ("y", "x"), 0, 0, tiled=True)
-    sums = partial_sums(got, own)
+    sums = partial_sums(got, own, done)
     got = lax.all_to_all(sums, "z", 0, 0, tiled=True)
     payload, own_sum, own_update = updates(got)
     mine = lax.all_to_all(payload, ("y", "x"), 0, 0, tiled=True)
     other = lax.ppermute(mine, "c", swap)
-    first_new, second_new = new_moments(block_ids, layer_ids, own_sum, first, second)
-    step_blocks, master_new = steps(block_ids, layer_ids, mine, other, own_update, master)
+    first_new, second_new = new_moments(hot, own_sum, first, second)
+    step_blocks, master_new = steps(layers, hot, mine, other, own_update, master)
     return (new_memory, master_new.T, first_new.T, second_new.T, step_blocks)
 
 

time: 66.6 us -> 66.1 us (level)
    ppermute x1, waiting for transfers between devices: 1.54 us -> 0.46 us  [on_device(): received = lax.ppermute(send, 'c', swap)]
    ppermute x1, waiting for transfers between devices: 0.04 us -> 0.71 us  [on_device(): other = lax.ppermute(mine, 'c', swap)]
    pallas_call x3 -> x4, Pallas kernels: 6.72 us -> 6.62 us  [the longest x1 2.79 us: pack_send(): pl.pallas_call(send_kernel, out_shape=(jax.ShapeDtypeStruct((1024, 128),...]
  transfers between devices with their start and end apart: 3 -> 3, of which waited for: 2 -> 3; matrix products, arithmetic and copies ran while one was open for 0% -> 0% of each run, Pallas kernels for 12% -> 13%
where the time goes in v3:
time: 66.1 us; the launch traced here: 65.7 us
  blocking collectives  32.9 us (50%)
  Pallas kernels  13.3 us (20%)
  starting transfers between devices  12.5 us (19%)
  waiting for transfers between devices  5.53 us (8%)
  other arithmetic  0.85 us (1%)
  between operations  0.7 us (1%)
    all_to_all x1, blocking collectives, on_device(): got = lax.all_to_all(sums, 'z', 0, 0, tiled=True)  19.1 us
    all_to_all x1, blocking collectives, on_device(): mine = lax.all_to_all(payload, ('y', 'x'), 0, 0, tiled=True)  13.8 us
    pallas_call x1, Pallas kernels, filter_memory(): pl.pallas_call(filter_kernel, out_shape=(jax.ShapeDtypeStruct(flat, jnp.b...  6.34 us
    all_to_all x1, starting transfers between devices, on_device(): got = lax.all_to_all(part, ('y', 'x'), 0, 0, tiled=True)  5.02 us
    all_to_all x1, waiting for transfers between devices, on_device(): got = lax.all_to_all(part, ('y', 'x'), 0, 0, tiled=True)  4.36 us
    ppermute x1, starting transfers between devices, on_device(): other = lax.ppermute(mine, 'c', swap)  4.12 us
    ppermute x1, starting transfers between devices, on_device(): received = lax.ppermute(send, 'c', swap)  3.33 us
    pallas_call x1, Pallas kernels, pack_send(): pl.pallas_call(send_kernel, out_shape=(jax.ShapeDtypeStruct((1024, 128),...  2.79 us
  transfers between devices with their start and end apart: 3, of which 3 were waited for; matrix products, arithmetic and copies ran while one was open for 0% of the time, Pallas kernels for 13%

profile of v3, /device:TPU:1, one launch (start us, length us, event | category | flops | bytes accessed | tf_op | source)
XLA Modules:
  0.0 65.7 jit_solution(6303194599447577311)
XLA Ops:
  0.6 0.0 copy-start
  0.6 0.0 copy-start.1
  0.7 0.0 copy-start.2
  0.7 2.8 %pack_send.1 = (f32[1024,128]{1,0:T(8,128)S(1)}, bf16[16,128,128]{2,1,0:T(8,128)(2,1)S(1)}, bf16[16,128,128]{2,1,0:T(8,128)(2,1)S(1)}) custom-call(s32[16]{0:T(128)} %block_ref.5, s32[16]{0:T(128)} %layer_ref.5, bf16[2,1024,1024]{2,1,0:T(8,128)(2,1)} %grads.1, bf16[2,1024,1024]{2,1,0:T(8,128)(2,1)} %memory.1), custom_call_target="tpu_custom_call" | custom-call | tf_op jit(solution)/shard_map/pack_send/pallas_call | solution.py:118
  3.5 3.3 %collective-permute-start = (f32[1024,128]{1,0:T(8,128)S(1)}, f32[1024,128]{1,0:T(8,128)S(1)}, u32[]{:S(2)}, u32[]{:S(2)}) collective-permute-start(f32[1024,128]{1,0:T(8,128)S(1)} %get-tuple-element.24), channel_id=1, source_target_pairs={{0,1},{1,0},{2,3},{3,2},{4,5},{5,4},{6,7},{7,6},{8,9},{9,8},{10,11... | collective-permute-start | bytes 1572872 | tf_op jit(solution)/shard_map/ppermute | solution.py:371
  6.8 0.0 copy-done
  6.8 0.0 copy-done.1
  6.8 0.0 copy-done.2
  6.8 1.1 %pack_keep.1 = (f32[1024,128]{1,0:T(8,128)S(1)}, f32[24,128]{1,0:T(8,128)S(1)}, f32[16,128]{1,0:T(8,128)S(1)}, s32[8,128]{1,0:T(8,128)S(1)}) custom-call(s32[16]{0:T(128)} %block_ref.5, s32[16]{0:T(128)} %layer_ref.5, bf16[16,128,128]{2,1,0:T(8,128)(2,1)S(1)} %get-tuple-element.21.g_tiles, bf16[16,128,128]{2,1,0:T(8,128)(2,1)S(1)} %get-tuple-element.22.m_tiles, ...), custom_call_target="tpu_custom_call" | custom-call | tf_op jit(solution)/shard_map/pack_keep/pallas_call | solution.py:134
  7.9 0.5 collective-permute-done
  8.3 0.8 %add.3 = f32[1024,128]{1,0:T(8,128)} add(f32[1024,128]{1,0:T(8,128)S(1)} %get-tuple-element.23, f32[1024,128]{1,0:T(8,128)S(1)} %collective-permute-done) | non-fusion elementwise | flops 131072 | bytes 1572864 | tf_op jit(solution)/shard_map/add | solution.py:373
  9.2 5.0 %all-to-all-start = ((f32[16,64,128]{2,1,0:T(8,128)}), f32[16,64,128]{2,1,0:T(8,128)S(1)}, u32[]{:S(2)}, u32[]{:S(2)}) async-start(f32[16,64,128]{2,1,0:T(8,128)} %bitcast.5.after), calls=%async_computation | async-start | bytes 1048576 | tf_op jit(solution)/shard_map/all_to_all | solution.py:375
  14.2 6.3 %filter_memory.1 = (bf16[2048,1024]{1,0:T(8,128)(2,1)}, f32[8,128]{1,0:T(8,128)S(1)}) custom-call(s32[16]{0:T(128)} %block_ref.5, s32[16]{0:T(128)} %layer_ref.5, bf16[2048,1024]{1,0:T(8,128)(2,1)} %bitcast.16, bf16[2048,1024]{1,0:T(8,128)(2,1)} %bitcast.17, f32[16,64,128]{2,1,0:T(8,128)} %bitcast.5.after), custom_call_target="tpu_custom_call" | custom-call | flops 8388608 | bytes 12582912 | tf_op jit(solution)/shard_map/filter_memory/pallas_call | solution.py:206
  20.6 4.4 %all-to-all-done.got = f32[16,64,128]{2,1,0:T(8,128)S(1)} async-done(((f32[16,64,128]{2,1,0:T(8,128)}), f32[16,64,128]{2,1,0:T(8,128)S(1)}, u32[]{:S(2)}, u32[]{:S(2)}) %all-to-all-start) | async-done | bytes 524320 | tf_op jit(solution)/shard_map/all_to_all | solution.py:375
  24.9 0.1 sum_partials.1
  25.0 19.1 %all_to_all.15.got = f32[8,88,128]{2,1,0:T(8,128)S(1)} all-to-all(f32[8,88,128]{2,1,0:T(8,128)S(1)} %sum_partials.1), channel_id=1, replica_groups=mesh['y'=4,'z'=8,'x'=4,'c'=2] {'z'}, dimensions={0} | all-to-all | bytes 720896 | tf_op jit(solution)/shard_map/all_to_all | solution.py:377
  44.0 0.3 lamb_update.1
  44.3 13.8 %all_to_all.16.own = f32[16,72,128]{2,1,0:T(8,128)S(1)} all-to-all(f32[16,72,128]{2,1,0:T(8,128)S(1)} %get-tuple-element.30), channel_id=1, replica_groups=mesh['y'=4,'z'=8,'x'=4,'c'=2] {'y','x'}, dimensions={0} | all-to-all | bytes 1179648 | tf_op jit(solution)/shard_map/all_to_all | solution.py:379
  58.1 4.1 %collective-permute-start.1 = (f32[16,72,128]{2,1,0:T(8,128)S(1)}, f32[16,72,128]{2,1,0:T(8,128)S(1)}, u32[]{:S(2)}, u32[]{:S(2)}) collective-permute-start(f32[16,72,128]{2,1,0:T(8,128)S(1)} %all_to_all.16.own), channel_id=1, source_target_pairs={{0,1},{1,0},{2,3},{3,2},{4,5},{5,4},{6,7},{7,6},{8,9},{9,8},{10,11... | collective-permute-start | bytes 1769480 | tf_op jit(solution)/shard_map/ppermute | solution.py:380
  62.2 0.9 %new_moments.1 = (f32[64,128]{1,0:T(8,128)}, f32[64,128]{1,0:T(8,128)}) custom-call(f32[16,128]{1,0:T(8,128)S(1)} %get-tuple-element.27.hot_ref, f32[8,128]{1,0:T(8,128)S(1)} %get-tuple-element.33.own_sum, f32[64,128]{1,0:T(8,128)S(1)} %bitcast.13, f32[64,128]{1,0:T(8,128)S(1)} %bitcast.15), custom_call_target="tpu_custom_call" | custom-call | tf_op jit(solution)/shard_map/new_moments/pallas_call | solution.py:293
  63.2 0.7 %collective-permute-done.1.other = f32[16,72,128]{2,1,0:T(8,128)S(1)} collective-permute-done((f32[16,72,128]{2,1,0:T(8,128)S(1)}, f32[16,72,128]{2,1,0:T(8,128)S(1)}, u32[]{:S(2)}, u32[]{:S(2)}) %collective-permute-start.1) | collective-permute-done | bytes 589856 | tf_op jit(solution)/shard_map/ppermute | solution.py:380
  63.9 1.8 %scaled_step.1 = (bf16[16,16384]{1,0:T(8,128)(2,1)}, f32[64,128]{1,0:T(8,128)}) custom-call(s32[8,128]{1,0:T(8,128)S(1)} %get-tuple-element.26.layers_ref, f32[16,128]{1,0:T(8,128)S(1)} %get-tuple-element.27.hot_ref, f32[16,72,128]{2,1,0:T(8,128)S(1)} %all_to_all.16.own, f32[16,72,128]{2,1,0:T(8,128)S(1)} %collective-permute-done.1.other, ...), custom_call_target="tpu_custom_call" | custom-call | tf_op jit(solution)/shard_map/scaled_step/pallas_call | solution.py:355
Async XLA Ops:
  0.6 6.2 %copy-start = (f32[128,64]{0,1:T(8,128)S(1)}, f32[128,64]{0,1:T(8,128)}, u32[]{:S(2)}) copy-start(f32[128,64]{0,1:T(8,128)} %param.11) | copy-start | bytes 98308
  0.6 6.2 %copy-start.1 = (f32[128,64]{0,1:T(8,128)S(1)}, f32[128,64]{0,1:T(8,128)}, u32[]{:S(2)}) copy-start(f32[128,64]{0,1:T(8,128)} %param.12) | copy-start | bytes 98308
  0.7 6.1 %copy-start.2 = (f32[128,64]{0,1:T(8,128)S(1)}, f32[128,64]{0,1:T(8,128)}, u32[]{:S(2)}) copy-start(f32[128,64]{0,1:T(8,128)} %param.13) | copy-start | bytes 98308
  3.5 4.9 %collective-permute-start = (f32[1024,128]{1,0:T(8,128)S(1)}, f32[1024,128]{1,0:T(8,128)S(1)}, u32[]{:S(2)}, u32[]{:S(2)}) collective-permute-start(f32[1024,128]{1,0:T(8,128)S(1)} %get-tuple-element.24), channel_id=1, source_target_pairs={{0,1},{1,0},{2,3},{3,2},{4,5},{5,4},{6,7},{7,6},{8,9},{9,8},{10,11... | collective-permute-start | bytes 1572872 | tf_op jit(solution)/shard_map/ppermute | solution.py:371
  9.2 15.7 %all-to-all-start = ((f32[16,64,128]{2,1,0:T(8,128)}), f32[16,64,128]{2,1,0:T(8,128)S(1)}, u32[]{:S(2)}, u32[]{:S(2)}) async-start(f32[16,64,128]{2,1,0:T(8,128)} %bitcast.5.after), calls=%async_computation | async-start | bytes 1048576 | tf_op jit(solution)/shard_map/all_to_all | solution.py:375
  58.1 5.8 %collective-permute-start.1 = (f32[16,72,128]{2,1,0:T(8,128)S(1)}, f32[16,72,128]{2,1,0:T(8,128)S(1)}, u32[]{:S(2)}, u32[]{:S(2)}) collective-permute-start(f32[16,72,128]{2,1,0:T(8,128)S(1)} %all_to_all.16.own), channel_id=1, source_target_pairs={{0,1},{1,0},{2,3},{3,2},{4,5},{5,4},{6,7},{7,6},{8,9},{9,8},{10,11... | collective-permute-start | bytes 1769480 | tf_op jit(solution)/shard_map/ppermute | solution.py:380

commit v4 on v3

--- a/solution.py
+++ b/solution.py
@@ -5,7 +5,6 @@
 from jax import lax
 from jax.experimental import pallas as pl
 from jax.experimental.pallas import tpu as pltpu
-from jax.sharding import Mesh
 from jax.sharding import PartitionSpec as P
 
 TILE = 128
@@ -24,6 +23,17 @@
 learn_rate = 0.01
 norm_eps = 1e-06
 
+
+def device(y, z, x, c):
+    return ((y * Z + z) * X + x) * C + c
+
+
+Z_ORDER = tuple(reversed(range(Z)))
+YX_ORDER = tuple((y, x) for y in reversed(range(Y)) for x in reversed(range(X)))
+Z_GROUPS = [[device(y, z, x, c) for z in Z_ORDER] for y in range(Y) for x in range(X) for c in range(C)]
+YX_GROUPS = [[device(y, z, x, c) for y, x in YX_ORDER] for z in range(Z) for c in range(C)]
+SWAP = [(i, i ^ 1) for i in range(Y * Z * X * C)]
+
 f32 = jnp.float32
 VMEM = pl.BlockSpec(memory_space=pltpu.VMEM)
 SMEM = pl.BlockSpec(memory_space=pltpu.SMEM)
@@ -83,7 +93,7 @@
     tmp[j] = value
     for y in range(Y):
         for x in range(X):
-            out_ref[pl.ds((y * X + x) * 64 + j * 8, 8), :] = tmp[j, pl.ds(y * Z * X + x, Z, stride=X), :]
+            out_ref[pl.ds(YX_ORDER.index((y, x)) * 64 + j * 8, 8), :] = tmp[j, pl.ds(y * Z * X + x, Z, stride=X), :]
 
 
 def send_kernel(block_ref, layer_ref, grads, memory, send_ref, g_tiles, m_tiles, tmp, g_sem, m_sem):
@@ -100,12 +110,12 @@
     for j in range(8):
         for copy in copies[4 * j : 4 * j + 4]:
             copy.wait()
-        store_rows(send_ref, tmp, j, half_columns(g_tiles, m_tiles, j, lax.axis_index("c") == 1))
+        store_rows(send_ref, tmp, j, half_columns(g_tiles, m_tiles, j, lax.axis_index("dp") % C == 1))
 
 
 def keep_kernel(block_ref, layer_ref, g_tiles, m_tiles, master, first, second, keep_ref, own_ref, hot_ref, layers_ref, tmp):
     for j in range(8):
-        store_rows(keep_ref, tmp, j, half_columns(g_tiles, m_tiles, j, lax.axis_index("c") == 0))
+        store_rows(keep_ref, tmp, j, half_columns(g_tiles, m_tiles, j, lax.axis_index("dp") % C == 0))
     hot = one_hot(block_ref, layer_ref)
     hot_ref[...] = hot
     layers_ref[...] = layer_tile(layer_ref)
@@ -240,16 +250,16 @@
 
 
 def update_kernel(got, out_ref, own_sum, own_update):
-    me = lax.axis_index("z")
+    me = lax.axis_index("dp") // (X * C) % Z
     squares = jnp.zeros((8, 128), f32)
     for z in range(Z):
         at = pl.ds(8 * z, 8)
         summed = got[0, at, :]
         for s in range(1, Z):
             summed = summed + got[s, at, :]
-        first = got[z, pl.ds(64, 8), :]
-        second = got[z, pl.ds(72, 8), :]
-        weights = got[z, pl.ds(80, 8), :]
+        first = got[Z_ORDER.index(z), pl.ds(64, 8), :]
+        second = got[Z_ORDER.index(z), pl.ds(72, 8), :]
+        weights = got[Z_ORDER.index(z), pl.ds(80, 8), :]
         first_sel = beta_one * first + (1.0 - beta_one) * summed
         second_sel = beta_two * second + (1.0 - beta_two) * summed * summed
         update = first_sel / (jnp.sqrt(second_sel) + adam_eps) + weight_decay * weights
@@ -322,7 +332,7 @@
         update_total = jnp.sum(jnp.where(mine, update_sq, 0.0), keepdims=True)
         ratio = jnp.where(mine, jnp.sqrt(weight_total / (update_total + norm_eps)), ratio)
     low = iota((8, 128), 1) < HALF
-    first_core = lax.axis_index("c") == 0
+    first_core = lax.axis_index("dp") % C == 0
 
     def chunk(i):
         at = pl.ds(i * WIDTH, WIDTH)
@@ -331,7 +341,7 @@
     for y in range(Y):
         for z in range(Z):
             for x in range(X):
-                at = (y * X + x, pl.ds(8 * z, 8))
+                at = (YX_ORDER.index((y, x)), pl.ds(8 * z, 8))
                 a = ratio * own[at]
                 b = ratio * other[at]
                 turned = pltpu.roll(jnp.where(first_core, b, a), HALF, 1)
@@ -364,33 +374,30 @@
 
 
 def on_device(grads, memory, block_ids, layer_ids, master, first_moment, second_moment):
-    swap = [(0, 1), (1, 0)]
     block_ids, layer_ids = in_hbm(block_ids), in_hbm(layer_ids)
     master, first, second = master.T, first_moment.T, second_moment.T
     send, g_tiles, m_tiles = pack_send(block_ids, layer_ids, grads, memory)
-    received = lax.ppermute(send, "c", swap)
+    received = lax.ppermute(send, "dp", SWAP)
     keep, own, hot, layers = pack_keep(block_ids, layer_ids, g_tiles, m_tiles, master, first, second)
     part = (keep + received).reshape(YX, 64, 128)
     new_memory, done = filter_memory(block_ids, layer_ids, grads, memory, part)
-    got = lax.all_to_all(part, ("y", "x"), 0, 0, tiled=True)
+    got = lax.all_to_all(part, "dp", 0, 0, axis_index_groups=YX_GROUPS, tiled=True)
     sums = partial_sums(got, own, done)
-    got = lax.all_to_all(sums, "z", 0, 0, tiled=True)
+    got = lax.all_to_all(sums, "dp", 0, 0, axis_index_groups=Z_GROUPS, tiled=True)
     payload, own_sum, own_update = updates(got)
-    mine = lax.all_to_all(payload, ("y", "x"), 0, 0, tiled=True)
-    other = lax.ppermute(mine, "c", swap)
+    mine = lax.all_to_all(payload, "dp", 0, 0, axis_index_groups=YX_GROUPS, tiled=True)
+    other = lax.ppermute(mine, "dp", SWAP)
     first_new, second_new = new_moments(hot, own_sum, first, second)
     step_blocks, master_new = steps(layers, hot, mine, other, own_update, master)
     return (new_memory, master_new.T, first_new.T, second_new.T, step_blocks)
 
 
 def solution(mesh):
-    torus = Mesh(mesh.devices.reshape(Y, Z, X, C), ("y", "z", "x", "c"))
-    dp = ("y", "z", "x", "c")
-    replica = P(dp, None, None)
-    state = P(None, dp)
+    replica = P("dp", None, None)
+    state = P(None, "dp")
     return jax.shard_map(
         on_device,
-        mesh=torus,
+        mesh=mesh,
         in_specs=(replica, replica, P(), P(), state, state, state),
         out_specs=(replica, state, state, state, P()),
         check_vma=False,

time: 66.1 us -> 61.5 us (0.930)
  blocking collectives: 32.9 us -> 29.5 us
  waiting for transfers between devices: 5.53 us -> 2.29 us
  starting transfers between devices: 12.5 us -> 14.2 us
    all_to_all x2, blocking collectives: 32.9 us -> 29.5 us  [the longest x1 16.5 us: on_device(): lax.all_to_all(sums, 'dp', 0, 0, axis_index_groups=Z_GROUPS, tiled=True)]
    all_to_all x1, waiting for transfers between devices: 4.36 us -> 1.13 us  [on_device(): lax.all_to_all(part, 'dp', 0, 0, axis_index_groups=YX_GROUPS, tiled=True)]
    all_to_all x1, starting transfers between devices: 5.02 us -> 6.65 us  [on_device(): lax.all_to_all(part, 'dp', 0, 0, axis_index_groups=YX_GROUPS, tiled=True)]
  transfers between devices with their start and end apart: 3 -> 3, of which waited for: 3 -> 3; matrix products, arithmetic and copies ran while one was open for 0% -> 0% of each run, Pallas kernels for 13% -> 14%
where the time goes in v4:
time: 61.5 us; the launch traced here: 60.8 us
  blocking collectives  29.5 us (48%)
  starting transfers between devices  14.2 us (23%)
  Pallas kernels  13.3 us (22%)
  waiting for transfers between devices  2.29 us (4%)
  other arithmetic  0.85 us (1%)
  between operations  0.69 us (1%)
    all_to_all x1, blocking collectives, on_device(): lax.all_to_all(sums, 'dp', 0, 0, axis_index_groups=Z_GROUPS, tiled=True)  16.5 us
    all_to_all x1, blocking collectives, on_device(): lax.all_to_all(payload, 'dp', 0, 0, axis_index_groups=YX_GROUPS, tiled=True)  13 us
    all_to_all x1, starting transfers between devices, on_device(): lax.all_to_all(part, 'dp', 0, 0, axis_index_groups=YX_GROUPS, tiled=True)  6.65 us
    pallas_call x1, Pallas kernels, filter_memory(): pl.pallas_call(filter_kernel, out_shape=(jax.ShapeDtypeStruct(flat, jnp.b...  6.34 us
    ppermute x1, starting transfers between devices, on_device(): other = lax.ppermute(mine, 'dp', SWAP)  4.24 us
    ppermute x1, starting transfers between devices, on_device(): received = lax.ppermute(send, 'dp', SWAP)  3.33 us
    pallas_call x1, Pallas kernels, pack_send(): pl.pallas_call(send_kernel, out_shape=(jax.ShapeDtypeStruct((1024, 128),...  2.8 us
    pallas_call x1, Pallas kernels, steps(): pl.pallas_call(step_kernel, out_shape=(jax.ShapeDtypeStruct(step, jnp.bfl...  1.84 us
  transfers between devices with their start and end apart: 3, of which 3 were waited for; matrix products, arithmetic and copies ran while one was open for 0% of the time, Pallas kernels for 14%

profile of v4, /device:TPU:1, one launch (start us, length us, event | category | flops | bytes accessed | tf_op | source)
XLA Modules:
  0.0 60.8 jit_solution(13334123798040512075)
XLA Ops:
  0.6 0.0 copy-start
  0.6 0.0 copy-start.1
  0.7 0.0 copy-start.2
  0.7 2.8 %pack_send.1 = (f32[1024,128]{1,0:T(8,128)S(1)}, bf16[16,128,128]{2,1,0:T(8,128)(2,1)S(1)}, bf16[16,128,128]{2,1,0:T(8,128)(2,1)S(1)}) custom-call(s32[16]{0:T(128)} %block_ref.5, s32[16]{0:T(128)} %layer_ref.5, bf16[2,1024,1024]{2,1,0:T(8,128)(2,1)} %grads.1, bf16[2,1024,1024]{2,1,0:T(8,128)(2,1)} %memory.1), custom_call_target="tpu_custom_call" | custom-call | tf_op jit(solution)/shard_map/pack_send/pallas_call | solution.py:128
  3.5 3.3 %collective-permute-start = (f32[1024,128]{1,0:T(8,128)S(1)}, f32[1024,128]{1,0:T(8,128)S(1)}, u32[]{:S(2)}, u32[]{:S(2)}) collective-permute-start(f32[1024,128]{1,0:T(8,128)S(1)} %get-tuple-element.24), channel_id=1, source_target_pairs={{0,1},{1,0},{2,3},{3,2},{4,5},{5,4},{6,7},{7,6},{8,9},{9,8},{10,11... | collective-permute-start | bytes 1572872 | tf_op jit(solution)/shard_map/ppermute | solution.py:380
  6.8 0.0 copy-done
  6.8 0.0 copy-done.1
  6.8 0.0 copy-done.2
  6.8 1.1 %pack_keep.1 = (f32[1024,128]{1,0:T(8,128)S(1)}, f32[24,128]{1,0:T(8,128)S(1)}, f32[16,128]{1,0:T(8,128)S(1)}, s32[8,128]{1,0:T(8,128)S(1)}) custom-call(s32[16]{0:T(128)} %block_ref.5, s32[16]{0:T(128)} %layer_ref.5, bf16[16,128,128]{2,1,0:T(8,128)(2,1)S(1)} %get-tuple-element.21.g_tiles, bf16[16,128,128]{2,1,0:T(8,128)(2,1)S(1)} %get-tuple-element.22.m_tiles, ...), custom_call_target="tpu_custom_call" | custom-call | tf_op jit(solution)/shard_map/pack_keep/pallas_call | solution.py:144
  7.9 0.5 collective-permute-done
  8.3 0.8 %add.3 = f32[1024,128]{1,0:T(8,128)} add(f32[1024,128]{1,0:T(8,128)S(1)} %get-tuple-element.23, f32[1024,128]{1,0:T(8,128)S(1)} %collective-permute-done) | non-fusion elementwise | flops 131072 | bytes 1572864 | tf_op jit(solution)/shard_map/add | solution.py:382
  9.2 6.7 %all-to-all-start = ((f32[16,64,128]{2,1,0:T(8,128)}), f32[16,64,128]{2,1,0:T(8,128)S(1)}, u32[]{:S(2)}, u32[]{:S(2)}) async-start(f32[16,64,128]{2,1,0:T(8,128)} %bitcast.5.after), calls=%async_computation | async-start | bytes 1048576 | tf_op jit(solution)/shard_map/all_to_all | solution.py:384
  15.8 6.3 %filter_memory.1 = (bf16[2048,1024]{1,0:T(8,128)(2,1)}, f32[8,128]{1,0:T(8,128)S(1)}) custom-call(s32[16]{0:T(128)} %block_ref.5, s32[16]{0:T(128)} %layer_ref.5, bf16[2048,1024]{1,0:T(8,128)(2,1)} %bitcast.16, bf16[2048,1024]{1,0:T(8,128)(2,1)} %bitcast.17, f32[16,64,128]{2,1,0:T(8,128)} %bitcast.5.after), custom_call_target="tpu_custom_call" | custom-call | flops 8388608 | bytes 12582912 | tf_op jit(solution)/shard_map/filter_memory/pallas_call | solution.py:216
  22.2 1.1 %all-to-all-done.got = f32[16,64,128]{2,1,0:T(8,128)S(1)} async-done(((f32[16,64,128]{2,1,0:T(8,128)}), f32[16,64,128]{2,1,0:T(8,128)S(1)}, u32[]{:S(2)}, u32[]{:S(2)}) %all-to-all-start) | async-done | bytes 524320 | tf_op jit(solution)/shard_map/all_to_all | solution.py:384
  23.3 0.1 sum_partials.1
  23.4 16.5 %all_to_all.15.got = f32[8,88,128]{2,1,0:T(8,128)S(1)} all-to-all(f32[8,88,128]{2,1,0:T(8,128)S(1)} %sum_partials.1), channel_id=1, replica_groups={{56,48,40,32,24,16,8,0},{57,49,41,33,25,17,9,1},{58,50,42,34,26,18,10,2..., dimensions={0} | all-to-all | bytes 720896 | tf_op jit(solution)/shard_map/all_to_all | solution.py:386
  39.9 0.3 lamb_update.1
  40.1 13.0 %all_to_all.16.own = f32[16,72,128]{2,1,0:T(8,128)S(1)} all-to-all(f32[16,72,128]{2,1,0:T(8,128)S(1)} %get-tuple-element.30), channel_id=1, replica_groups={{198,196,194,192,134,132,130,128,70,68,66,64,6,4,2,0},{199,197,195,193,..., dimensions={0} | all-to-all | bytes 1179648 | tf_op jit(solution)/shard_map/all_to_all | solution.py:388
  53.1 4.2 %collective-permute-start.1 = (f32[16,72,128]{2,1,0:T(8,128)S(1)}, f32[16,72,128]{2,1,0:T(8,128)S(1)}, u32[]{:S(2)}, u32[]{:S(2)}) collective-permute-start(f32[16,72,128]{2,1,0:T(8,128)S(1)} %all_to_all.16.own), channel_id=1, source_target_pairs={{0,1},{1,0},{2,3},{3,2},{4,5},{5,4},{6,7},{7,6},{8,9},{9,8},{10,11... | collective-permute-start | bytes 1769480 | tf_op jit(solution)/shard_map/ppermute | solution.py:389
  57.4 0.9 %new_moments.1 = (f32[64,128]{1,0:T(8,128)}, f32[64,128]{1,0:T(8,128)}) custom-call(f32[16,128]{1,0:T(8,128)S(1)} %get-tuple-element.27.hot_ref, f32[8,128]{1,0:T(8,128)S(1)} %get-tuple-element.33.own_sum, f32[64,128]{1,0:T(8,128)S(1)} %bitcast.13, f32[64,128]{1,0:T(8,128)S(1)} %bitcast.15), custom_call_target="tpu_custom_call" | custom-call | tf_op jit(solution)/shard_map/new_moments/pallas_call | solution.py:303
  58.3 0.7 %collective-permute-done.1.other = f32[16,72,128]{2,1,0:T(8,128)S(1)} collective-permute-done((f32[16,72,128]{2,1,0:T(8,128)S(1)}, f32[16,72,128]{2,1,0:T(8,128)S(1)}, u32[]{:S(2)}, u32[]{:S(2)}) %collective-permute-start.1) | collective-permute-done | bytes 589856 | tf_op jit(solution)/shard_map/ppermute | solution.py:389
  59.0 1.8 %scaled_step.1 = (bf16[16,16384]{1,0:T(8,128)(2,1)}, f32[64,128]{1,0:T(8,128)}) custom-call(s32[8,128]{1,0:T(8,128)S(1)} %get-tuple-element.26.layers_ref, f32[16,128]{1,0:T(8,128)S(1)} %get-tuple-element.27.hot_ref, f32[16,72,128]{2,1,0:T(8,128)S(1)} %all_to_all.16.own, f32[16,72,128]{2,1,0:T(8,128)S(1)} %collective-permute-done.1.other, ...), custom_call_target="tpu_custom_call" | custom-call | tf_op jit(solution)/shard_map/scaled_step/pallas_call | solution.py:365
Async XLA Ops:
  0.6 6.2 %copy-start = (f32[128,64]{0,1:T(8,128)S(1)}, f32[128,64]{0,1:T(8,128)}, u32[]{:S(2)}) copy-start(f32[128,64]{0,1:T(8,128)} %param.11) | copy-start | bytes 98308
  0.6 6.2 %copy-start.1 = (f32[128,64]{0,1:T(8,128)S(1)}, f32[128,64]{0,1:T(8,128)}, u32[]{:S(2)}) copy-start(f32[128,64]{0,1:T(8,128)} %param.12) | copy-start | bytes 98308
  0.7 6.2 %copy-start.2 = (f32[128,64]{0,1:T(8,128)S(1)}, f32[128,64]{0,1:T(8,128)}, u32[]{:S(2)}) copy-start(f32[128,64]{0,1:T(8,128)} %param.13) | copy-start | bytes 98308
  3.5 4.9 %collective-permute-start = (f32[1024,128]{1,0:T(8,128)S(1)}, f32[1024,128]{1,0:T(8,128)S(1)}, u32[]{:S(2)}, u32[]{:S(2)}) collective-permute-start(f32[1024,128]{1,0:T(8,128)S(1)} %get-tuple-element.24), channel_id=1, source_target_pairs={{0,1},{1,0},{2,3},{3,2},{4,5},{5,4},{6,7},{7,6},{8,9},{9,8},{10,11... | collective-permute-start | bytes 1572872 | tf_op jit(solution)/shard_map/ppermute | solution.py:380
  9.2 14.1 %all-to-all-start = ((f32[16,64,128]{2,1,0:T(8,128)}), f32[16,64,128]{2,1,0:T(8,128)S(1)}, u32[]{:S(2)}, u32[]{:S(2)}) async-start(f32[16,64,128]{2,1,0:T(8,128)} %bitcast.5.after), calls=%async_computation | async-start | bytes 1048576 | tf_op jit(solution)/shard_map/all_to_all | solution.py:384
  53.1 5.9 %collective-permute-start.1 = (f32[16,72,128]{2,1,0:T(8,128)S(1)}, f32[16,72,128]{2,1,0:T(8,128)S(1)}, u32[]{:S(2)}, u32[]{:S(2)}) collective-permute-start(f32[16,72,128]{2,1,0:T(8,128)S(1)} %all_to_all.16.own), channel_id=1, source_target_pairs={{0,1},{1,0},{2,3},{3,2},{4,5},{5,4},{6,7},{7,6},{8,9},{9,8},{10,11... | collective-permute-start | bytes 1769480 | tf_op jit(solution)/shard_map/ppermute | solution.py:389

commit v5 on v4

--- a/solution.py
+++ b/solution.py
@@ -90,7 +90,7 @@
 
 
 def store_rows(out_ref, tmp, j, value):
-    tmp[j] = value
+    tmp[j, pl.ds(0, TILE), :] = value
     for y in range(Y):
         for x in range(X):
             out_ref[pl.ds(YX_ORDER.index((y, x)) * 64 + j * 8, 8), :] = tmp[j, pl.ds(y * Z * X + x, Z, stride=X), :]
@@ -131,7 +131,7 @@
         in_specs=[SMEM, SMEM, HBM, HBM],
         out_specs=(VMEM, VMEM, VMEM),
         scratch_shapes=[
-            pltpu.VMEM((8, TILE, TILE), f32),
+            pltpu.VMEM((8, TILE + 8, TILE), f32),
             pltpu.SemaphoreType.DMA((SEL,)),
             pltpu.SemaphoreType.DMA((SEL,)),
         ],
@@ -151,7 +151,7 @@
         ),
         in_specs=[SMEM, SMEM, VMEM, VMEM, VMEM, VMEM, VMEM],
         out_specs=(VMEM, VMEM, VMEM, VMEM),
-        scratch_shapes=[pltpu.VMEM((8, TILE, TILE), f32)],
+        scratch_shapes=[pltpu.VMEM((8, TILE + 8, TILE), f32)],
         compiler_params=SMALL,
         name="pack_keep",
     )(block_ids, layer_ids, g_tiles, m_tiles, master, first, second)
@@ -233,7 +233,7 @@
             total = total + got[s, pl.ds(8 * j, 8), :]
         tmp[pl.ds(j, Z, stride=8), :] = total
     for z in range(Z):
-        out_ref[z, pl.ds(0, 64), :] = tmp[...]
+        out_ref[z, pl.ds(0, 64), :] = tmp[pl.ds(0, 64), :]
         out_ref[z, pl.ds(64, 24), :] = own[...]
 
 
@@ -243,7 +243,7 @@
         out_shape=jax.ShapeDtypeStruct((Z, 88, 128), f32),
         in_specs=[VMEM, VMEM, VMEM],
         out_specs=VMEM,
-        scratch_shapes=[pltpu.VMEM((64, 128), f32)],
+        scratch_shapes=[pltpu.VMEM((72, 128), f32)],
         compiler_params=SMALL,
         name="sum_partials",
     )(got, own, after)

time: 61.5 us -> 61.5 us (level)
  no operation moved by 1% of the time
where the time goes in v5:
time: 61.5 us; the launch traced here: 60.8 us
  blocking collectives  29.5 us (48%)
  starting transfers between devices  14.2 us (23%)
  Pallas kernels  13.3 us (22%)
  waiting for transfers between devices  2.29 us (4%)
  other arithmetic  0.85 us (1%)
  between operations  0.69 us (1%)
    all_to_all x1, blocking collectives, on_device(): lax.all_to_all(sums, 'dp', 0, 0, axis_index_groups=Z_GROUPS, tiled=True)  16.5 us
    all_to_all x1, blocking collectives, on_device(): lax.all_to_all(payload, 'dp', 0, 0, axis_index_groups=YX_GROUPS, tiled=True)  13 us
    all_to_all x1, starting transfers between devices, on_device(): lax.all_to_all(part, 'dp', 0, 0, axis_index_groups=YX_GROUPS, tiled=True)  6.65 us
    pallas_call x1, Pallas kernels, filter_memory(): pl.pallas_call(filter_kernel, out_shape=(jax.ShapeDtypeStruct(flat, jnp.b...  6.34 us
    ppermute x1, starting transfers between devices, on_device(): other = lax.ppermute(mine, 'dp', SWAP)  4.24 us
    ppermute x1, starting transfers between devices, on_device(): received = lax.ppermute(send, 'dp', SWAP)  3.33 us
    pallas_call x1, Pallas kernels, pack_send(): pl.pallas_call(send_kernel, out_shape=(jax.ShapeDtypeStruct((1024, 128),...  2.8 us
    pallas_call x1, Pallas kernels, steps(): pl.pallas_call(step_kernel, out_shape=(jax.ShapeDtypeStruct(step, jnp.bfl...  1.84 us
  transfers between devices with their start and end apart: 3, of which 3 were waited for; matrix products, arithmetic and copies ran while one was open for 0% of the time, Pallas kernels for 14%

profile of v5, /device:TPU:1, one launch (start us, length us, event | category | flops | bytes accessed | tf_op | source)
XLA Modules:
  0.0 60.8 jit_solution(17638827374883880300)
XLA Ops:
  0.6 0.0 copy-start
  0.6 0.0 copy-start.1
  0.7 0.0 copy-start.2
  0.7 2.8 %pack_send.1 = (f32[1024,128]{1,0:T(8,128)S(1)}, bf16[16,128,128]{2,1,0:T(8,128)(2,1)S(1)}, bf16[16,128,128]{2,1,0:T(8,128)(2,1)S(1)}) custom-call(s32[16]{0:T(128)} %block_ref.5, s32[16]{0:T(128)} %layer_ref.5, bf16[2,1024,1024]{2,1,0:T(8,128)(2,1)} %grads.1, bf16[2,1024,1024]{2,1,0:T(8,128)(2,1)} %memory.1), custom_call_target="tpu_custom_call" | custom-call | tf_op jit(solution)/shard_map/pack_send/pallas_call | solution.py:128
  3.5 3.3 %collective-permute-start = (f32[1024,128]{1,0:T(8,128)S(1)}, f32[1024,128]{1,0:T(8,128)S(1)}, u32[]{:S(2)}, u32[]{:S(2)}) collective-permute-start(f32[1024,128]{1,0:T(8,128)S(1)} %get-tuple-element.24), channel_id=1, source_target_pairs={{0,1},{1,0},{2,3},{3,2},{4,5},{5,4},{6,7},{7,6},{8,9},{9,8},{10,11... | collective-permute-start | bytes 1572872 | tf_op jit(solution)/shard_map/ppermute | solution.py:380
  6.8 0.0 copy-done
  6.8 0.0 copy-done.1
  6.8 0.0 copy-done.2
  6.8 1.1 %pack_keep.1 = (f32[1024,128]{1,0:T(8,128)S(1)}, f32[24,128]{1,0:T(8,128)S(1)}, f32[16,128]{1,0:T(8,128)S(1)}, s32[8,128]{1,0:T(8,128)S(1)}) custom-call(s32[16]{0:T(128)} %block_ref.5, s32[16]{0:T(128)} %layer_ref.5, bf16[16,128,128]{2,1,0:T(8,128)(2,1)S(1)} %get-tuple-element.21.g_tiles, bf16[16,128,128]{2,1,0:T(8,128)(2,1)S(1)} %get-tuple-element.22.m_tiles, ...), custom_call_target="tpu_custom_call" | custom-call | tf_op jit(solution)/shard_map/pack_keep/pallas_call | solution.py:144
  7.9 0.5 collective-permute-done
  8.3 0.8 %add.3 = f32[1024,128]{1,0:T(8,128)} add(f32[1024,128]{1,0:T(8,128)S(1)} %get-tuple-element.23, f32[1024,128]{1,0:T(8,128)S(1)} %collective-permute-done) | non-fusion elementwise | flops 131072 | bytes 1572864 | tf_op jit(solution)/shard_map/add | solution.py:382
  9.2 6.7 %all-to-all-start = ((f32[16,64,128]{2,1,0:T(8,128)}), f32[16,64,128]{2,1,0:T(8,128)S(1)}, u32[]{:S(2)}, u32[]{:S(2)}) async-start(f32[16,64,128]{2,1,0:T(8,128)} %bitcast.5.after), calls=%async_computation | async-start | bytes 1048576 | tf_op jit(solution)/shard_map/all_to_all | solution.py:384
  15.8 6.3 %filter_memory.1 = (bf16[2048,1024]{1,0:T(8,128)(2,1)}, f32[8,128]{1,0:T(8,128)S(1)}) custom-call(s32[16]{0:T(128)} %block_ref.5, s32[16]{0:T(128)} %layer_ref.5, bf16[2048,1024]{1,0:T(8,128)(2,1)} %bitcast.16, bf16[2048,1024]{1,0:T(8,128)(2,1)} %bitcast.17, f32[16,64,128]{2,1,0:T(8,128)} %bitcast.5.after), custom_call_target="tpu_custom_call" | custom-call | flops 8388608 | bytes 12582912 | tf_op jit(solution)/shard_map/filter_memory/pallas_call | solution.py:216
  22.2 1.1 %all-to-all-done.got = f32[16,64,128]{2,1,0:T(8,128)S(1)} async-done(((f32[16,64,128]{2,1,0:T(8,128)}), f32[16,64,128]{2,1,0:T(8,128)S(1)}, u32[]{:S(2)}, u32[]{:S(2)}) %all-to-all-start) | async-done | bytes 524320 | tf_op jit(solution)/shard_map/all_to_all | solution.py:384
  23.3 0.1 sum_partials.1
  23.4 16.5 %all_to_all.15.got = f32[8,88,128]{2,1,0:T(8,128)S(1)} all-to-all(f32[8,88,128]{2,1,0:T(8,128)S(1)} %sum_partials.1), channel_id=1, replica_groups={{56,48,40,32,24,16,8,0},{57,49,41,33,25,17,9,1},{58,50,42,34,26,18,10,2..., dimensions={0} | all-to-all | bytes 720896 | tf_op jit(solution)/shard_map/all_to_all | solution.py:386
  39.9 0.3 lamb_update.1
  40.1 13.0 %all_to_all.16.own = f32[16,72,128]{2,1,0:T(8,128)S(1)} all-to-all(f32[16,72,128]{2,1,0:T(8,128)S(1)} %get-tuple-element.30), channel_id=1, replica_groups={{198,196,194,192,134,132,130,128,70,68,66,64,6,4,2,0},{199,197,195,193,..., dimensions={0} | all-to-all | bytes 1179648 | tf_op jit(solution)/shard_map/all_to_all | solution.py:388
  53.1 4.2 %collective-permute-start.1 = (f32[16,72,128]{2,1,0:T(8,128)S(1)}, f32[16,72,128]{2,1,0:T(8,128)S(1)}, u32[]{:S(2)}, u32[]{:S(2)}) collective-permute-start(f32[16,72,128]{2,1,0:T(8,128)S(1)} %all_to_all.16.own), channel_id=1, source_target_pairs={{0,1},{1,0},{2,3},{3,2},{4,5},{5,4},{6,7},{7,6},{8,9},{9,8},{10,11... | collective-permute-start | bytes 1769480 | tf_op jit(solution)/shard_map/ppermute | solution.py:389
  57.4 0.9 %new_moments.1 = (f32[64,128]{1,0:T(8,128)}, f32[64,128]{1,0:T(8,128)}) custom-call(f32[16,128]{1,0:T(8,128)S(1)} %get-tuple-element.27.hot_ref, f32[8,128]{1,0:T(8,128)S(1)} %get-tuple-element.33.own_sum, f32[64,128]{1,0:T(8,128)S(1)} %bitcast.13, f32[64,128]{1,0:T(8,128)S(1)} %bitcast.15), custom_call_target="tpu_custom_call" | custom-call | tf_op jit(solution)/shard_map/new_moments/pallas_call | solution.py:303
  58.3 0.7 %collective-permute-done.1.other = f32[16,72,128]{2,1,0:T(8,128)S(1)} collective-permute-done((f32[16,72,128]{2,1,0:T(8,128)S(1)}, f32[16,72,128]{2,1,0:T(8,128)S(1)}, u32[]{:S(2)}, u32[]{:S(2)}) %collective-permute-start.1) | collective-permute-done | bytes 589856 | tf_op jit(solution)/shard_map/ppermute | solution.py:389
  59.0 1.8 %scaled_step.1 = (bf16[16,16384]{1,0:T(8,128)(2,1)}, f32[64,128]{1,0:T(8,128)}) custom-call(s32[8,128]{1,0:T(8,128)S(1)} %get-tuple-element.26.layers_ref, f32[16,128]{1,0:T(8,128)S(1)} %get-tuple-element.27.hot_ref, f32[16,72,128]{2,1,0:T(8,128)S(1)} %all_to_all.16.own, f32[16,72,128]{2,1,0:T(8,128)S(1)} %collective-permute-done.1.other, ...), custom_call_target="tpu_custom_call" | custom-call | tf_op jit(solution)/shard_map/scaled_step/pallas_call | solution.py:365
Async XLA Ops:
  0.6 6.2 %copy-start = (f32[128,64]{0,1:T(8,128)S(1)}, f32[128,64]{0,1:T(8,128)}, u32[]{:S(2)}) copy-start(f32[128,64]{0,1:T(8,128)} %param.11) | copy-start | bytes 98308
  0.6 6.2 %copy-start.1 = (f32[128,64]{0,1:T(8,128)S(1)}, f32[128,64]{0,1:T(8,128)}, u32[]{:S(2)}) copy-start(f32[128,64]{0,1:T(8,128)} %param.12) | copy-start | bytes 98308
  0.7 6.1 %copy-start.2 = (f32[128,64]{0,1:T(8,128)S(1)}, f32[128,64]{0,1:T(8,128)}, u32[]{:S(2)}) copy-start(f32[128,64]{0,1:T(8,128)} %param.13) | copy-start | bytes 98308
  3.5 4.9 %collective-permute-start = (f32[1024,128]{1,0:T(8,128)S(1)}, f32[1024,128]{1,0:T(8,128)S(1)}, u32[]{:S(2)}, u32[]{:S(2)}) collective-permute-start(f32[1024,128]{1,0:T(8,128)S(1)} %get-tuple-element.24), channel_id=1, source_target_pairs={{0,1},{1,0},{2,3},{3,2},{4,5},{5,4},{6,7},{7,6},{8,9},{9,8},{10,11... | collective-permute-start | bytes 1572872 | tf_op jit(solution)/shard_map/ppermute | solution.py:380
  9.2 14.1 %all-to-all-start = ((f32[16,64,128]{2,1,0:T(8,128)}), f32[16,64,128]{2,1,0:T(8,128)S(1)}, u32[]{:S(2)}, u32[]{:S(2)}) async-start(f32[16,64,128]{2,1,0:T(8,128)} %bitcast.5.after), calls=%async_computation | async-start | bytes 1048576 | tf_op jit(solution)/shard_map/all_to_all | solution.py:384
  53.1 5.9 %collective-permute-start.1 = (f32[16,72,128]{2,1,0:T(8,128)S(1)}, f32[16,72,128]{2,1,0:T(8,128)S(1)}, u32[]{:S(2)}, u32[]{:S(2)}) collective-permute-start(f32[16,72,128]{2,1,0:T(8,128)S(1)} %all_to_all.16.own), channel_id=1, source_target_pairs={{0,1},{1,0},{2,3},{3,2},{4,5},{5,4},{6,7},{7,6},{8,9},{9,8},{10,11... | collective-permute-start | bytes 1769480 | tf_op jit(solution)/shard_map/ppermute | solution.py:389

commit v6 on v5

--- a/solution.py
+++ b/solution.py
@@ -226,30 +226,33 @@
     return out.reshape(2, 1024, 1024), done
 
 
-def partial_kernel(got, own, after, out_ref, tmp):
+def partial_kernel(got, own, out_ref, tmp, sem):
     for j in range(8):
         total = got[0, pl.ds(8 * j, 8), :]
         for s in range(1, YX):
             total = total + got[s, pl.ds(8 * j, 8), :]
         tmp[pl.ds(j, Z, stride=8), :] = total
-    for z in range(Z):
-        out_ref[z, pl.ds(0, 64), :] = tmp[pl.ds(0, 64), :]
-        out_ref[z, pl.ds(64, 24), :] = own[...]
-
-
-def partial_sums(got, own, after):
+    tmp[pl.ds(64, 24), :] = own[...]
+    copies = [pltpu.make_async_copy(tmp.at[pl.ds(0, 88)], out_ref.at[z], sem.at[z]) for z in range(Z)]
+    for copy in copies:
+        copy.start()
+    for copy in copies:
+        copy.wait()
+
+
+def partial_sums(got, own):
     return pl.pallas_call(
         partial_kernel,
         out_shape=jax.ShapeDtypeStruct((Z, 88, 128), f32),
-        in_specs=[VMEM, VMEM, VMEM],
-        out_specs=VMEM,
-        scratch_shapes=[pltpu.VMEM((72, 128), f32)],
+        in_specs=[VMEM, VMEM],
+        out_specs=HBM,
+        scratch_shapes=[pltpu.VMEM((88, 128), f32), pltpu.SemaphoreType.DMA((Z,))],
         compiler_params=SMALL,
         name="sum_partials",
-    )(got, own, after)
-
-
-def update_kernel(got, out_ref, own_sum, own_update):
+    )(got, own)
+
+
+def update_kernel(got, after, out_ref, own_sum, own_update):
     me = lax.axis_index("dp") // (X * C) % Z
     squares = jnp.zeros((8, 128), f32)
     for z in range(Z):
@@ -276,16 +279,16 @@
         out_ref[s, pl.ds(64, 8), :] = squares
 
 
-def updates(got):
+def updates(got, after):
     tile = jax.ShapeDtypeStruct((8, 128), f32)
     return pl.pallas_call(
         update_kernel,
         out_shape=(jax.ShapeDtypeStruct((YX, 72, 128), f32), tile, tile),
-        in_specs=[VMEM],
+        in_specs=[VMEM, VMEM],
         out_specs=(VMEM, VMEM, VMEM),
         compiler_params=SMALL,
         name="lamb_update",
-    )(got)
+    )(got, after)
 
 
 def state_kernel(hot_ref, own_sum, first, second, first_new, second_new):
@@ -380,11 +383,11 @@
     received = lax.ppermute(send, "dp", SWAP)
     keep, own, hot, layers = pack_keep(block_ids, layer_ids, g_tiles, m_tiles, master, first, second)
     part = (keep + received).reshape(YX, 64, 128)
-    new_memory, done = filter_memory(block_ids, layer_ids, grads, memory, part)
     got = lax.all_to_all(part, "dp", 0, 0, axis_index_groups=YX_GROUPS, tiled=True)
-    sums = partial_sums(got, own, done)
+    sums = partial_sums(got, own)
+    new_memory, done = filter_memory(block_ids, layer_ids, grads, memory, sums)
     got = lax.all_to_all(sums, "dp", 0, 0, axis_index_groups=Z_GROUPS, tiled=True)
-    payload, own_sum, own_update = updates(got)
+    payload, own_sum, own_update = updates(got, done)
     mine = lax.all_to_all(payload, "dp", 0, 0, axis_index_groups=YX_GROUPS, tiled=True)
     other = lax.ppermute(mine, "dp", SWAP)
     first_new, second_new = new_moments(hot, own_sum, first, second)

time: 61.5 us -> 61.3 us (level)
  the two profiles are of different devices: /device:TPU:1 before, /device:TPU:33 now
where the time goes in v6:
time: 61.3 us; the launch traced here: 60.9 us
  blocking collectives  29.1 us (47%)
  Pallas kernels  14.1 us (23%)
  starting transfers between devices  12 us (20%)
  waiting for transfers between devices  4.98 us (8%)
  between operations  0.7 us (1%)
    all_to_all x1, blocking collectives, on_device(): lax.all_to_all(part, 'dp', 0, 0, axis_index_groups=YX_GROUPS, tiled=True)  15 us
    all_to_all x1, blocking collectives, on_device(): lax.all_to_all(payload, 'dp', 0, 0, axis_index_groups=YX_GROUPS, tiled=True)  14.1 us
    all_to_all x1, starting transfers between devices, on_device(): lax.all_to_all(sums, 'dp', 0, 0, axis_index_groups=Z_GROUPS, tiled=True)  8.51 us
    pallas_call x1, Pallas kernels, filter_memory(): pl.pallas_call(filter_kernel, out_shape=(jax.ShapeDtypeStruct(flat, jnp.b...  6.34 us
    all_to_all x1, waiting for transfers between devices, on_device(): lax.all_to_all(sums, 'dp', 0, 0, axis_index_groups=Z_GROUPS, tiled=True)  3.82 us
    pallas_call x1, Pallas kernels, pack_send(): pl.pallas_call(send_kernel, out_shape=(jax.ShapeDtypeStruct((1024, 128),...  2.8 us
    ppermute x1, starting transfers between devices, on_device(): other = lax.ppermute(mine, 'dp', SWAP)  2.71 us
    pallas_call x1, Pallas kernels, steps(): pl.pallas_call(step_kernel, out_shape=(jax.ShapeDtypeStruct(step, jnp.bfl...  1.84 us
  transfers between devices with their start and end apart: 3, of which 3 were waited for; matrix products, arithmetic and copies ran while one was open for 0% of the time, Pallas kernels for 14%

profile of v6, /device:TPU:33, one launch (start us, length us, event | category | flops | bytes accessed | tf_op | source)
XLA Modules:
  0.0 60.9 jit_solution(7668162529524185002)
XLA Ops:
  0.6 0.0 copy-start
  0.6 0.0 copy-start.1
  0.7 0.0 copy-start.2
  0.7 2.8 %pack_send.1 = (f32[1024,128]{1,0:T(8,128)S(1)}, bf16[16,128,128]{2,1,0:T(8,128)(2,1)S(1)}, bf16[16,128,128]{2,1,0:T(8,128)(2,1)S(1)}) custom-call(s32[16]{0:T(128)} %block_ref.5, s32[16]{0:T(128)} %layer_ref.5, bf16[2,1024,1024]{2,1,0:T(8,128)(2,1)} %grads.1, bf16[2,1024,1024]{2,1,0:T(8,128)(2,1)} %memory.1), custom_call_target="tpu_custom_call" | custom-call | tf_op jit(solution)/shard_map/pack_send/pallas_call | solution.py:128
  3.5 0.8 %collective-permute-start = (f32[1024,128]{1,0:T(8,128)S(1)}, f32[1024,128]{1,0:T(8,128)S(1)}, u32[]{:S(2)}, u32[]{:S(2)}) collective-permute-start(f32[1024,128]{1,0:T(8,128)S(1)} %get-tuple-element.24), channel_id=1, source_target_pairs={{0,1},{1,0},{2,3},{3,2},{4,5},{5,4},{6,7},{7,6},{8,9},{9,8},{10,11... | collective-permute-start | bytes 1572872 | tf_op jit(solution)/shard_map/ppermute | solution.py:383
  4.2 0.0 copy-done
  4.2 0.0 copy-done.1
  4.2 0.0 copy-done.2
  4.2 1.1 %pack_keep.1 = (f32[1024,128]{1,0:T(8,128)S(1)}, f32[24,128]{1,0:T(8,128)S(1)}, f32[16,128]{1,0:T(8,128)S(1)}, s32[8,128]{1,0:T(8,128)S(1)}) custom-call(s32[16]{0:T(128)} %block_ref.5, s32[16]{0:T(128)} %layer_ref.5, bf16[16,128,128]{2,1,0:T(8,128)(2,1)S(1)} %get-tuple-element.21.g_tiles, bf16[16,128,128]{2,1,0:T(8,128)(2,1)S(1)} %get-tuple-element.22.m_tiles, ...), custom_call_target="tpu_custom_call" | custom-call | tf_op jit(solution)/shard_map/pack_keep/pallas_call | solution.py:144
  5.3 0.5 collective-permute-done
  5.8 0.1 add.3
  5.8 15.0 %all_to_all.15.got = f32[16,64,128]{2,1,0:T(8,128)S(1)} all-to-all(f32[16,64,128]{2,1,0:T(8,128)S(1)} %bitcast.18), channel_id=1, replica_groups={{198,196,194,192,134,132,130,128,70,68,66,64,6,4,2,0},{199,197,195,193,..., dimensions={0} | all-to-all | bytes 1048576 | tf_op jit(solution)/shard_map/all_to_all | solution.py:386
  20.9 0.8 %sum_partials.1.after = f32[8,88,128]{2,1,0:T(8,128)} custom-call(f32[16,64,128]{2,1,0:T(8,128)S(1)} %all_to_all.15.got, f32[24,128]{1,0:T(8,128)S(1)} %get-tuple-element.25.own), custom_call_target="tpu_custom_call" | custom-call | tf_op jit(solution)/shard_map/sum_partials/pallas_call | solution.py:244
  21.7 8.5 %all-to-all-start.1 = ((f32[8,88,128]{2,1,0:T(8,128)}), f32[8,88,128]{2,1,0:T(8,128)S(1)}, u32[]{:S(2)}, u32[]{:S(2)}) async-start(f32[8,88,128]{2,1,0:T(8,128)} %sum_partials.1.after), calls=%async_computation.1 | async-start | bytes 720896 | tf_op jit(solution)/shard_map/all_to_all | solution.py:389
  30.2 6.3 %filter_memory.1 = (bf16[2048,1024]{1,0:T(8,128)(2,1)}, f32[8,128]{1,0:T(8,128)S(1)}) custom-call(s32[16]{0:T(128)} %block_ref.5, s32[16]{0:T(128)} %layer_ref.5, bf16[2048,1024]{1,0:T(8,128)(2,1)} %bitcast.16, bf16[2048,1024]{1,0:T(8,128)(2,1)} %bitcast.17, f32[8,88,128]{2,1,0:T(8,128)} %sum_partials.1.after), custom_call_target="tpu_custom_call" | custom-call | flops 8388608 | bytes 12582912 | tf_op jit(solution)/shard_map/filter_memory/pallas_call | solution.py:216
  36.5 3.8 %all-to-all-done.1.got = f32[8,88,128]{2,1,0:T(8,128)S(1)} async-done(((f32[8,88,128]{2,1,0:T(8,128)}), f32[8,88,128]{2,1,0:T(8,128)S(1)}, u32[]{:S(2)}, u32[]{:S(2)}) %all-to-all-start.1) | async-done | bytes 360480 | tf_op jit(solution)/shard_map/all_to_all | solution.py:389
  40.4 0.3 lamb_update.1
  40.6 14.1 %all_to_all.16.own = f32[16,72,128]{2,1,0:T(8,128)S(1)} all-to-all(f32[16,72,128]{2,1,0:T(8,128)S(1)} %get-tuple-element.30), channel_id=1, replica_groups={{198,196,194,192,134,132,130,128,70,68,66,64,6,4,2,0},{199,197,195,193,..., dimensions={0} | all-to-all | bytes 1179648 | tf_op jit(solution)/shard_map/all_to_all | solution.py:391
  54.7 2.7 %collective-permute-start.1 = (f32[16,72,128]{2,1,0:T(8,128)S(1)}, f32[16,72,128]{2,1,0:T(8,128)S(1)}, u32[]{:S(2)}, u32[]{:S(2)}) collective-permute-start(f32[16,72,128]{2,1,0:T(8,128)S(1)} %all_to_all.16.own), channel_id=1, source_target_pairs={{0,1},{1,0},{2,3},{3,2},{4,5},{5,4},{6,7},{7,6},{8,9},{9,8},{10,11... | collective-permute-start | bytes 1769480 | tf_op jit(solution)/shard_map/ppermute | solution.py:392
  57.4 0.9 %new_moments.1 = (f32[64,128]{1,0:T(8,128)}, f32[64,128]{1,0:T(8,128)}) custom-call(f32[16,128]{1,0:T(8,128)S(1)} %get-tuple-element.28.hot_ref, f32[8,128]{1,0:T(8,128)S(1)} %get-tuple-element.33.own_sum, f32[64,128]{1,0:T(8,128)S(1)} %bitcast.13, f32[64,128]{1,0:T(8,128)S(1)} %bitcast.15), custom_call_target="tpu_custom_call" | custom-call | tf_op jit(solution)/shard_map/new_moments/pallas_call | solution.py:306
  58.3 0.7 %collective-permute-done.1.other = f32[16,72,128]{2,1,0:T(8,128)S(1)} collective-permute-done((f32[16,72,128]{2,1,0:T(8,128)S(1)}, f32[16,72,128]{2,1,0:T(8,128)S(1)}, u32[]{:S(2)}, u32[]{:S(2)}) %collective-permute-start.1) | collective-permute-done | bytes 589856 | tf_op jit(solution)/shard_map/ppermute | solution.py:392
  59.1 1.8 %scaled_step.1 = (bf16[16,16384]{1,0:T(8,128)(2,1)}, f32[64,128]{1,0:T(8,128)}) custom-call(s32[8,128]{1,0:T(8,128)S(1)} %get-tuple-element.27.layers_ref, f32[16,128]{1,0:T(8,128)S(1)} %get-tuple-element.28.hot_ref, f32[16,72,128]{2,1,0:T(8,128)S(1)} %all_to_all.16.own, f32[16,72,128]{2,1,0:T(8,128)S(1)} %collective-permute-done.1.other, ...), custom_call_target="tpu_custom_call" | custom-call | tf_op jit(solution)/shard_map/scaled_step/pallas_call | solution.py:368
Async XLA Ops:
  0.6 3.6 %copy-start = (f32[128,64]{0,1:T(8,128)S(1)}, f32[128,64]{0,1:T(8,128)}, u32[]{:S(2)}) copy-start(f32[128,64]{0,1:T(8,128)} %param.11) | copy-start | bytes 98308
  0.6 3.6 %copy-start.1 = (f32[128,64]{0,1:T(8,128)S(1)}, f32[128,64]{0,1:T(8,128)}, u32[]{:S(2)}) copy-start(f32[128,64]{0,1:T(8,128)} %param.12) | copy-start | bytes 98308
  0.7 3.6 %copy-start.2 = (f32[128,64]{0,1:T(8,128)S(1)}, f32[128,64]{0,1:T(8,128)}, u32[]{:S(2)}) copy-start(f32[128,64]{0,1:T(8,128)} %param.13) | copy-start | bytes 98308
  3.5 2.3 %collective-permute-start = (f32[1024,128]{1,0:T(8,128)S(1)}, f32[1024,128]{1,0:T(8,128)S(1)}, u32[]{:S(2)}, u32[]{:S(2)}) collective-permute-start(f32[1024,128]{1,0:T(8,128)S(1)} %get-tuple-element.24), channel_id=1, source_target_pairs={{0,1},{1,0},{2,3},{3,2},{4,5},{5,4},{6,7},{7,6},{8,9},{9,8},{10,11... | collective-permute-start | bytes 1572872 | tf_op jit(solution)/shard_map/ppermute | solution.py:383
  21.7 18.7 %all-to-all-start.1 = ((f32[8,88,128]{2,1,0:T(8,128)}), f32[8,88,128]{2,1,0:T(8,128)S(1)}, u32[]{:S(2)}, u32[]{:S(2)}) async-start(f32[8,88,128]{2,1,0:T(8,128)} %sum_partials.1.after), calls=%async_computation.1 | async-start | bytes 720896 | tf_op jit(solution)/shard_map/all_to_all | solution.py:389
  54.7 4.3 %collective-permute-start.1 = (f32[16,72,128]{2,1,0:T(8,128)S(1)}, f32[16,72,128]{2,1,0:T(8,128)S(1)}, u32[]{:S(2)}, u32[]{:S(2)}) collective-permute-start(f32[16,72,128]{2,1,0:T(8,128)S(1)} %all_to_all.16.own), channel_id=1, source_target_pairs={{0,1},{1,0},{2,3},{3,2},{4,5},{5,4},{6,7},{7,6},{8,9},{9,8},{10,11... | collective-permute-start | bytes 1769480 | tf_op jit(solution)/shard_map/ppermute | solution.py:392

commit v7 on v6

--- a/solution.py
+++ b/solution.py
@@ -28,7 +28,7 @@
     return ((y * Z + z) * X + x) * C + c
 
 
-Z_ORDER = tuple(reversed(range(Z)))
+Z_ORDER = (7, 6, 5, 4, 3, 1, 2, 0)
 YX_ORDER = tuple((y, x) for y in reversed(range(Y)) for x in reversed(range(X)))
 Z_GROUPS = [[device(y, z, x, c) for z in Z_ORDER] for y in range(Y) for x in range(X) for c in range(C)]
 YX_GROUPS = [[device(y, z, x, c) for y, x in YX_ORDER] for z in range(Z) for c in range(C)]

time: 61.3 us -> 61.2 us (level)
  the two profiles are of different devices: /device:TPU:33 before, /device:TPU:1 now
where the time goes in v7:
time: 61.2 us; the launch traced here: 60.7 us
  blocking collectives  26.5 us (43%)
  starting transfers between devices  18.1 us (30%)
  Pallas kernels  14 us (23%)
  waiting for transfers between devices  1.22 us (2%)
  between operations  0.7 us (1%)
    all_to_all x1, blocking collectives, on_device(): lax.all_to_all(part, 'dp', 0, 0, axis_index_groups=YX_GROUPS, tiled=True)  13.3 us
    all_to_all x1, blocking collectives, on_device(): lax.all_to_all(payload, 'dp', 0, 0, axis_index_groups=YX_GROUPS, tiled=True)  13.2 us
    all_to_all x1, starting transfers between devices, on_device(): lax.all_to_all(sums, 'dp', 0, 0, axis_index_groups=Z_GROUPS, tiled=True)  8.97 us
    pallas_call x1, Pallas kernels, filter_memory(): pl.pallas_call(filter_kernel, out_shape=(jax.ShapeDtypeStruct(flat, jnp.b...  6.34 us
    ppermute x1, starting transfers between devices, on_device(): other = lax.ppermute(mine, 'dp', SWAP)  5.84 us
    ppermute x1, starting transfers between devices, on_device(): received = lax.ppermute(send, 'dp', SWAP)  3.33 us
    pallas_call x1, Pallas kernels, pack_send(): pl.pallas_call(send_kernel, out_shape=(jax.ShapeDtypeStruct((1024, 128),...  2.79 us
    pallas_call x1, Pallas kernels, steps(): pl.pallas_call(step_kernel, out_shape=(jax.ShapeDtypeStruct(step, jnp.bfl...  1.84 us
  transfers between devices with their start and end apart: 3, of which 3 were waited for; matrix products, arithmetic and copies ran while one was open for 0% of the time, Pallas kernels for 14%

profile of v7, /device:TPU:1, one launch (start us, length us, event | category | flops | bytes accessed | tf_op | source)
XLA Modules:
  0.0 60.7 jit_solution(7653909677111405857)
XLA Ops:
  0.6 0.0 copy-start
  0.6 0.0 copy-start.1
  0.7 0.0 copy-start.2
  0.7 2.8 %pack_send.1 = (f32[1024,128]{1,0:T(8,128)S(1)}, bf16[16,128,128]{2,1,0:T(8,128)(2,1)S(1)}, bf16[16,128,128]{2,1,0:T(8,128)(2,1)S(1)}) custom-call(s32[16]{0:T(128)} %block_ref.5, s32[16]{0:T(128)} %layer_ref.5, bf16[2,1024,1024]{2,1,0:T(8,128)(2,1)} %grads.1, bf16[2,1024,1024]{2,1,0:T(8,128)(2,1)} %memory.1), custom_call_target="tpu_custom_call" | custom-call | tf_op jit(solution)/shard_map/pack_send/pallas_call | solution.py:128
  3.5 3.3 %collective-permute-start = (f32[1024,128]{1,0:T(8,128)S(1)}, f32[1024,128]{1,0:T(8,128)S(1)}, u32[]{:S(2)}, u32[]{:S(2)}) collective-permute-start(f32[1024,128]{1,0:T(8,128)S(1)} %get-tuple-element.24), channel_id=1, source_target_pairs={{0,1},{1,0},{2,3},{3,2},{4,5},{5,4},{6,7},{7,6},{8,9},{9,8},{10,11... | collective-permute-start | bytes 1572872 | tf_op jit(solution)/shard_map/ppermute | solution.py:383
  6.8 0.0 copy-done
  6.8 0.0 copy-done.1
  6.8 0.0 copy-done.2
  6.8 1.1 %pack_keep.1 = (f32[1024,128]{1,0:T(8,128)S(1)}, f32[24,128]{1,0:T(8,128)S(1)}, f32[16,128]{1,0:T(8,128)S(1)}, s32[8,128]{1,0:T(8,128)S(1)}) custom-call(s32[16]{0:T(128)} %block_ref.5, s32[16]{0:T(128)} %layer_ref.5, bf16[16,128,128]{2,1,0:T(8,128)(2,1)S(1)} %get-tuple-element.21.g_tiles, bf16[16,128,128]{2,1,0:T(8,128)(2,1)S(1)} %get-tuple-element.22.m_tiles, ...), custom_call_target="tpu_custom_call" | custom-call | tf_op jit(solution)/shard_map/pack_keep/pallas_call | solution.py:144
  7.9 0.5 collective-permute-done
  8.3 0.1 add.3
  8.4 13.3 %all_to_all.15.got = f32[16,64,128]{2,1,0:T(8,128)S(1)} all-to-all(f32[16,64,128]{2,1,0:T(8,128)S(1)} %bitcast.18), channel_id=1, replica_groups={{198,196,194,192,134,132,130,128,70,68,66,64,6,4,2,0},{199,197,195,193,..., dimensions={0} | all-to-all | bytes 1048576 | tf_op jit(solution)/shard_map/all_to_all | solution.py:386
  21.7 0.8 %sum_partials.1.after = f32[8,88,128]{2,1,0:T(8,128)} custom-call(f32[16,64,128]{2,1,0:T(8,128)S(1)} %all_to_all.15.got, f32[24,128]{1,0:T(8,128)S(1)} %get-tuple-element.25.own), custom_call_target="tpu_custom_call" | custom-call | tf_op jit(solution)/shard_map/sum_partials/pallas_call | solution.py:244
  22.5 9.0 %all-to-all-start.1 = ((f32[8,88,128]{2,1,0:T(8,128)}), f32[8,88,128]{2,1,0:T(8,128)S(1)}, u32[]{:S(2)}, u32[]{:S(2)}) async-start(f32[8,88,128]{2,1,0:T(8,128)} %sum_partials.1.after), calls=%async_computation.1 | async-start | bytes 720896 | tf_op jit(solution)/shard_map/all_to_all | solution.py:389
  31.5 6.3 %filter_memory.1 = (bf16[2048,1024]{1,0:T(8,128)(2,1)}, f32[8,128]{1,0:T(8,128)S(1)}) custom-call(s32[16]{0:T(128)} %block_ref.5, s32[16]{0:T(128)} %layer_ref.5, bf16[2048,1024]{1,0:T(8,128)(2,1)} %bitcast.16, bf16[2048,1024]{1,0:T(8,128)(2,1)} %bitcast.17, f32[8,88,128]{2,1,0:T(8,128)} %sum_partials.1.after), custom_call_target="tpu_custom_call" | custom-call | flops 8388608 | bytes 12582912 | tf_op jit(solution)/shard_map/filter_memory/pallas_call | solution.py:216
  37.8 0.1 all-to-all-done.1.got
  37.9 0.3 lamb_update.1
  38.2 13.2 %all_to_all.16.own = f32[16,72,128]{2,1,0:T(8,128)S(1)} all-to-all(f32[16,72,128]{2,1,0:T(8,128)S(1)} %get-tuple-element.30), channel_id=1, replica_groups={{198,196,194,192,134,132,130,128,70,68,66,64,6,4,2,0},{199,197,195,193,..., dimensions={0} | all-to-all | bytes 1179648 | tf_op jit(solution)/shard_map/all_to_all | solution.py:391
  51.4 5.8 %collective-permute-start.1 = (f32[16,72,128]{2,1,0:T(8,128)S(1)}, f32[16,72,128]{2,1,0:T(8,128)S(1)}, u32[]{:S(2)}, u32[]{:S(2)}) collective-permute-start(f32[16,72,128]{2,1,0:T(8,128)S(1)} %all_to_all.16.own), channel_id=1, source_target_pairs={{0,1},{1,0},{2,3},{3,2},{4,5},{5,4},{6,7},{7,6},{8,9},{9,8},{10,11... | collective-permute-start | bytes 1769480 | tf_op jit(solution)/shard_map/ppermute | solution.py:392
  57.2 0.9 %new_moments.1 = (f32[64,128]{1,0:T(8,128)}, f32[64,128]{1,0:T(8,128)}) custom-call(f32[16,128]{1,0:T(8,128)S(1)} %get-tuple-element.28.hot_ref, f32[8,128]{1,0:T(8,128)S(1)} %get-tuple-element.33.own_sum, f32[64,128]{1,0:T(8,128)S(1)} %bitcast.13, f32[64,128]{1,0:T(8,128)S(1)} %bitcast.15), custom_call_target="tpu_custom_call" | custom-call | tf_op jit(solution)/shard_map/new_moments/pallas_call | solution.py:306
  58.2 0.7 %collective-permute-done.1.other = f32[16,72,128]{2,1,0:T(8,128)S(1)} collective-permute-done((f32[16,72,128]{2,1,0:T(8,128)S(1)}, f32[16,72,128]{2,1,0:T(8,128)S(1)}, u32[]{:S(2)}, u32[]{:S(2)}) %collective-permute-start.1) | collective-permute-done | bytes 589856 | tf_op jit(solution)/shard_map/ppermute | solution.py:392
  58.9 1.8 %scaled_step.1 = (bf16[16,16384]{1,0:T(8,128)(2,1)}, f32[64,128]{1,0:T(8,128)}) custom-call(s32[8,128]{1,0:T(8,128)S(1)} %get-tuple-element.27.layers_ref, f32[16,128]{1,0:T(8,128)S(1)} %get-tuple-element.28.hot_ref, f32[16,72,128]{2,1,0:T(8,128)S(1)} %all_to_all.16.own, f32[16,72,128]{2,1,0:T(8,128)S(1)} %collective-permute-done.1.other, ...), custom_call_target="tpu_custom_call" | custom-call | tf_op jit(solution)/shard_map/scaled_step/pallas_call | solution.py:368
Async XLA Ops:
  0.6 6.2 %copy-start = (f32[128,64]{0,1:T(8,128)S(1)}, f32[128,64]{0,1:T(8,128)}, u32[]{:S(2)}) copy-start(f32[128,64]{0,1:T(8,128)} %param.11) | copy-start | bytes 98308
  0.6 6.1 %copy-start.1 = (f32[128,64]{0,1:T(8,128)S(1)}, f32[128,64]{0,1:T(8,128)}, u32[]{:S(2)}) copy-start(f32[128,64]{0,1:T(8,128)} %param.12) | copy-start | bytes 98308
  0.7 6.1 %copy-start.2 = (f32[128,64]{0,1:T(8,128)S(1)}, f32[128,64]{0,1:T(8,128)}, u32[]{:S(2)}) copy-start(f32[128,64]{0,1:T(8,128)} %param.13) | copy-start | bytes 98308
  3.5 4.9 %collective-permute-start = (f32[1024,128]{1,0:T(8,128)S(1)}, f32[1024,128]{1,0:T(8,128)S(1)}, u32[]{:S(2)}, u32[]{:S(2)}) collective-permute-start(f32[1024,128]{1,0:T(8,128)S(1)} %get-tuple-element.24), channel_id=1, source_target_pairs={{0,1},{1,0},{2,3},{3,2},{4,5},{5,4},{6,7},{7,6},{8,9},{9,8},{10,11... | collective-permute-start | bytes 1572872 | tf_op jit(solution)/shard_map/ppermute | solution.py:383
  22.5 15.4 %all-to-all-start.1 = ((f32[8,88,128]{2,1,0:T(8,128)}), f32[8,88,128]{2,1,0:T(8,128)S(1)}, u32[]{:S(2)}, u32[]{:S(2)}) async-start(f32[8,88,128]{2,1,0:T(8,128)} %sum_partials.1.after), calls=%async_computation.1 | async-start | bytes 720896 | tf_op jit(solution)/shard_map/all_to_all | solution.py:389
  51.4 7.5 %collective-permute-start.1 = (f32[16,72,128]{2,1,0:T(8,128)S(1)}, f32[16,72,128]{2,1,0:T(8,128)S(1)}, u32[]{:S(2)}, u32[]{:S(2)}) collective-permute-start(f32[16,72,128]{2,1,0:T(8,128)S(1)} %all_to_all.16.own), channel_id=1, source_target_pairs={{0,1},{1,0},{2,3},{3,2},{4,5},{5,4},{6,7},{7,6},{8,9},{9,8},{10,11... | collective-permute-start | bytes 1769480 | tf_op jit(solution)/shard_map/ppermute | solution.py:392
